TPU v7x, 256 devices: a whole 4x4x8 slice. The times are simulated.
256 devices in a mesh: dp: 8 (over z_lo, core), ctx: 32 (over y, x, z_hi).
Axes of the slice: x: 4, y: 4, z: 8 (z_hi: 2, z_lo: 4; z = z_hi * 4 + z_lo), core: 2. Of those that a mesh axis runs over, the one named last changes fastest.
Arguments:
- layer_input: bfloat16 [8, 4096, 16384], P('dp', 'ctx'), may hold values from -6 to 6
- query_rows: bfloat16 [8, 4096, 1024], P('dp', 'ctx'), may hold values from -512 to 512
- key_rows: bfloat16 [8, 4096, 128], P('dp', 'ctx'), may hold values from -5 to 5
- value_rows: bfloat16 [8, 4096, 128], P('dp', 'ctx'), may hold values from -6 to 6
- out_grad: bfloat16 [8, 4096, 1024], P('dp', 'ctx'), may hold values from -6 to 6
- block_order: int32 [64], replicated, may hold values from 0 to 63, each once
- master: float32 [16384, 1280], P(('dp', 'ctx')), may hold values from -3 to 3
- moment_one: float32 [16384, 1280], P(('dp', 'ctx')), may hold values from -6 to 6
- moment_two: float32 [16384, 1280], P(('dp', 'ctx')), may hold values from 0.5 to 20
Outputs:
- new_master: float32 [16384, 1280], P(('dp', 'ctx'))
- new_moment_one: float32 [16384, 1280], P(('dp', 'ctx'))
- new_moment_two: float32 [16384, 1280], P(('dp', 'ctx'))
Inputs may be any that keep to these rules, and one draw needn't show every extreme that they name: Stored rows j * 64 to (j + 1) * 64 - 1 of every sequence hold positions block_order[j] * 64 onward, in order; each of the 64 blocks appears once.
All inputs are finite; a program needn't handle non-finite values.
Results may differ from a plain program's by a relative error of at most 0.0048.
Values may be sent and summed in bfloat16 or wider, within the bound.
A program may use at most 64 MiB of HBM per device.

v0:
```python
import math

import jax
import jax.numpy as jnp
from jax import lax
from jax.sharding import PartitionSpec as P

STEP = 10


NEG_FILL = -1e30
BETA_ONE = 0.9
BETA_TWO = 0.95
EPSILON = 1e-08
LEARN_RATE = 0.01
DECAY = 0.1
ROW_CONTRACT = (((1,), (1,)), ((), ()))
COL_CONTRACT = (((0,), (0,)), ((), ()))


def forward_block(carried, key_blk, value_blk, key_pos, rows_q, rows_o, query_pos, score_scale):
    max_old, total_old, inner_old = carried
    scores = (
        lax.dot_general(rows_q, key_blk, ROW_CONTRACT, preferred_element_type=jnp.float32)
        * score_scale
    )
    grad_prob = lax.dot_general(rows_o, value_blk, ROW_CONTRACT, preferred_element_type=jnp.float32)
    visible = key_pos[None, :] <= query_pos[:, None]
    max_new = jnp.maximum(max_old, jnp.max(jnp.where(visible, scores, NEG_FILL), axis=1))
    weights = jnp.where(visible, jnp.exp(scores - max_new[:, None]), 0.0)
    factor = jnp.exp(max_old - max_new)
    return (
        max_new,
        total_old * factor + jnp.sum(weights, axis=1),
        inner_old * factor + jnp.sum(weights * grad_prob, axis=1),
    )


def forward_over(
    carried, key_all, value_all, key_pos_all, rows_q, rows_o, query_pos, score_scale, block_size
):
    key_count = key_all.shape[0]
    blk_rows = math.gcd(key_count, block_size)
    blk_count = key_count // blk_rows

    def forward_advance(state_now, block_items):
        key_blk, value_blk, key_pos = block_items
        return (
            forward_block(
                state_now, key_blk, value_blk, key_pos, rows_q, rows_o, query_pos, score_scale
            ),
            None,
        )

    result, unused_out = lax.scan(
        forward_advance,
        carried,
        (
            key_all.reshape(blk_count, blk_rows, -1),
            value_all.reshape(blk_count, blk_rows, -1),
            key_pos_all.reshape(blk_count, blk_rows),
        ),
    )
    return result


def backward_over(
    key_all, value_all, key_pos_all, rows_q, rows_o, query_pos, log_total, delta_row, score_scale
):
    key_count, head_dim = key_all.shape
    blk_rows = math.gcd(key_count, 512)
    blk_count = key_count // blk_rows

    def backward_advance(dq_acc, block_items):
        key_blk, value_blk, key_pos = block_items
        scores = (
            lax.dot_general(rows_q, key_blk, ROW_CONTRACT, preferred_element_type=jnp.float32)
            * score_scale
        )
        visible = key_pos[None, :] <= query_pos[:, None]
        prob_full = jnp.where(visible, jnp.exp(scores - log_total[:, None]), 0.0)
        grad_prob = lax.dot_general(
            rows_o, value_blk, ROW_CONTRACT, preferred_element_type=jnp.float32
        )
        dscore = (prob_full * (grad_prob - delta_row[:, None]) * score_scale).astype(jnp.bfloat16)
        prob_low = prob_full.astype(jnp.bfloat16)
        acc_out = dq_acc + jnp.dot(dscore, key_blk, preferred_element_type=jnp.float32)
        key_term = lax.dot_general(dscore, rows_q, COL_CONTRACT, preferred_element_type=jnp.float32)
        value_term = lax.dot_general(
            prob_low, rows_o, COL_CONTRACT, preferred_element_type=jnp.float32
        )
        return (acc_out, jnp.concatenate([key_term, value_term], axis=1))

    start_acc = jnp.zeros((rows_q.shape[0], head_dim), jnp.float32)
    dq_final, key_terms = lax.scan(
        backward_advance,
        start_acc,
        (
            key_all.reshape(blk_count, blk_rows, -1),
            value_all.reshape(blk_count, blk_rows, -1),
            key_pos_all.reshape(blk_count, blk_rows),
        ),
    )
    return (dq_final, key_terms.reshape(key_count, 2 * head_dim))


def per_device(
    layer_input,
    query_rows,
    key_rows,
    value_rows,
    out_grad,
    block_order,
    master,
    moment_one,
    moment_two,
):
    tok_rows = query_rows.shape[1]
    q_width = query_rows.shape[2]
    head_dim = key_rows.shape[2]
    group_size = q_width // head_dim
    half_rows = tok_rows // 2
    block_count = block_order.shape[0]
    seq_length = block_count * half_rows
    dp_count = lax.axis_size("dp")
    ctx_count = lax.axis_size("ctx")
    own_rows = master.shape[0]
    score_scale = 1.0 / math.sqrt(head_dim)
    pos_all = (
        block_order[:, None] * half_rows + jnp.arange(half_rows, dtype=jnp.int32)[None, :]
    ).reshape(seq_length)
    ctx_rank = lax.axis_index("ctx")
    my_pos = lax.dynamic_slice_in_dim(pos_all, ctx_rank * tok_rows, tok_rows)
    query_pos = jnp.repeat(my_pos, group_size)
    rows_q = query_rows[0].reshape(tok_rows * group_size, head_dim)
    rows_o = out_grad[0].reshape(tok_rows * group_size, head_dim)
    keys_here = key_rows[0]
    values_here = value_rows[0]
    pieces = layer_input[0].reshape(tok_rows, dp_count, ctx_count, own_rows)
    received = lax.all_to_all(pieces, "ctx", split_axis=2, concat_axis=0, tiled=True)
    columns = received.reshape(seq_length, dp_count * own_rows)
    row_total = tok_rows * group_size
    start_state = (
        jnp.full((row_total,), NEG_FILL, jnp.float32),
        jnp.zeros((row_total,), jnp.float32),
        jnp.zeros((row_total,), jnp.float32),
    )
    fold_size = 512
    max_run, total_run, inner_run = forward_over(
        start_state,
        lax.all_gather(keys_here, "ctx", axis=0, tiled=True),
        lax.all_gather(values_here, "ctx", axis=0, tiled=True),
        pos_all,
        rows_q,
        rows_o,
        query_pos,
        score_scale,
        fold_size,
    )
    key_all, value_all = (
        lax.all_gather(keys_here, "ctx", axis=0, tiled=True),
        lax.all_gather(values_here, "ctx", axis=0, tiled=True),
    )
    log_total = max_run + jnp.log(total_run)
    delta_row = inner_run / total_run
    dq_final, key_terms = backward_over(
        key_all, value_all, pos_all, rows_q, rows_o, query_pos, log_total, delta_row, score_scale
    )
    dq_local = dq_final.astype(jnp.bfloat16).reshape(tok_rows, q_width)
    kv_mine = lax.psum_scatter(key_terms, "ctx", scatter_dimension=0, tiled=True).astype(
        jnp.bfloat16
    )
    dq_all, kv_full = (
        lax.all_gather(dq_local, "ctx", axis=0, tiled=True),
        lax.all_gather(kv_mine, "ctx", axis=0, tiled=True),
    )
    query_part = lax.dot_general(columns, dq_all, COL_CONTRACT, preferred_element_type=jnp.float32)
    key_part = lax.dot_general(columns, kv_full, COL_CONTRACT, preferred_element_type=jnp.float32)
    grad_local = lax.psum_scatter(
        jnp.concatenate([query_part, key_part], axis=1), "dp", scatter_dimension=0, tiled=True
    )
    new_one = BETA_ONE * moment_one + (1.0 - BETA_ONE) * grad_local
    new_two = BETA_TWO * moment_two + (1.0 - BETA_TWO) * grad_local * grad_local
    corr_one = 1.0 - BETA_ONE**STEP
    corr_two = 1.0 - BETA_TWO**STEP
    update = new_one / corr_one / (jnp.sqrt(new_two / corr_two) + EPSILON)
    new_master = master - LEARN_RATE * (update + DECAY * master)
    return (new_master, new_one, new_two)


def solution(mesh):
    in_specs = (
        P("dp", "ctx", None),
        P("dp", "ctx", None),
        P("dp", "ctx", None),
        P("dp", "ctx", None),
        P("dp", "ctx", None),
        P(),
        P(("dp", "ctx"), None),
        P(("dp", "ctx"), None),
        P(("dp", "ctx"), None),
    )
    out_specs = (P(("dp", "ctx"), None), P(("dp", "ctx"), None), P(("dp", "ctx"), None))
    return jax.shard_map(
        per_device, mesh=mesh, in_specs=in_specs, out_specs=out_specs, check_vma=False
    )
```

profile of v0, /device:TPU:1, one launch (start us, length us, event | category | flops | bytes accessed | tf_op | source)
XLA Modules:
  0.0 891.0 jit_solution(96315023097437728)
XLA Ops:
  12.1 83.3 %all-gather.11.cloned.1.call-done = bf16[1,4096,128]{2,1,0:T(8,128)(2,1)} async-done(((bf16[1,128,128]{2,1,0:T(8,128)(2,1)}), bf16[1,4096,128]{2,1,0:T(8,128)(2,1)}) %all-gather.11.cloned.1.call-update) | async-done | bytes 1048592 | tf_op jit(solution)/shard_map/all_gather | solution.py:161
  95.4 79.2 %all-gather.13.cloned.1.call-done = bf16[1,4096,128]{2,1,0:T(8,128)(2,1)} async-done(((bf16[1,128,128]{2,1,0:T(8,128)(2,1)}), bf16[1,4096,128]{2,1,0:T(8,128)(2,1)}) %all-gather.13.cloned.1.call-update) | async-done | bytes 1048592 | tf_op jit(solution)/shard_map/all_gather | solution.py:162
  174.6 29.9 %while.28 = (s32[]{:T(128)}, f32[1024]{0:T(1024)S(1)}, f32[1024]{0:T(1024)S(1)}, f32[1024]{0:T(1024)S(1)}, s32[8,512]{1,0:T(8,128)S(1)}, /*index=5*/bf16[8,512,1...) while((s32[]{:T(128)}, f32[1024]{0:T(1024)S(1)}, ...), condition=%wide.region_4.5_spmd.clone, body=%wide.region_0.4_spmd.clone.sunk | while | flops 276306944 | bytes 7187092 | solution.py:55
  174.8 1.4 fusion.79
  176.2 1.6 fusion.80
  178.6 1.4 fusion.79
  180.0 1.6 fusion.80
  182.3 1.4 fusion.79
  183.7 1.6 fusion.80
  186.0 1.4 fusion.79
  187.4 1.6 fusion.80
  189.8 1.4 fusion.79
  191.2 1.6 fusion.80
  193.5 1.4 fusion.79
  194.9 1.6 fusion.80
  197.3 1.4 fusion.79
  198.7 1.6 fusion.80
  201.0 1.4 fusion.79
  202.4 1.6 fusion.80
  204.5 67.7 %while.29 = (s32[]{:T(128)}, f32[1024,128]{1,0:T(8,128)}, f32[8,512,256]{2,1,0:T(8,128)}, s32[8,512]{1,0:T(8,128)S(1)}, bf16[8,512,128]{2,1,0:T(8,128)(2,1)}, /*...) while((s32[]{:T(128)}, f32[1024,128]{1,0:T(8,128)}, ...), condition=%wide.region_6.7_spmd.clone, body=%wide.region_5.6_spmd.clone.sunk | while | flops 676200448 | bytes 17726172 | solution.py:95
  204.8 1.5 bitcast_select_fusion.2
  206.3 1.3 fusion.93
  207.6 2.2 convolution_add_fusion.2
  210.3 1.4 fusion.95
  213.0 1.5 bitcast_select_fusion.2
  214.5 1.3 fusion.93
  215.9 2.4 convolution_add_fusion.2
  218.8 1.4 fusion.95
  221.5 1.5 bitcast_select_fusion.2
  223.0 1.3 fusion.93
  224.4 2.4 convolution_add_fusion.2
  227.3 1.4 fusion.95
  230.0 1.5 bitcast_select_fusion.2
  231.5 1.3 fusion.93
  232.9 2.4 convolution_add_fusion.2
  235.8 1.4 fusion.95
  238.5 1.5 bitcast_select_fusion.2
  240.0 1.3 fusion.93
  241.4 2.4 convolution_add_fusion.2
  244.3 1.4 fusion.95
  247.0 1.5 bitcast_select_fusion.2
  249.9 2.4 convolution_add_fusion.2
  252.7 1.4 fusion.95
  255.5 1.5 bitcast_select_fusion.2
  257.0 1.3 fusion.93
  258.4 2.4 convolution_add_fusion.2
  261.2 1.4 fusion.95
  264.0 1.5 bitcast_select_fusion.2
  265.5 1.3 fusion.93
  266.8 2.4 convolution_add_fusion.2
  269.7 1.4 fusion.95
  272.3 237.7 %reduce-scatter.5.cloned.1.call-done = f32[128,256]{1,0:T(8,128)} async-done(((f32[4096,256]{1,0:T(8,128)}), f32[128,256]{1,0:T(8,128)}) %reduce-scatter.5.cloned.1.call-update) | async-done | bytes 131088 | tf_op jit(solution)/shard_map/reduce_scatter | solution.py:170
  510.0 1.5 convert_element_type.13
  512.6 6.4 copy.40
  519.0 3.1 copy.41
  522.1 44.4 %all_to_all.15 = bf16[128,8,32,64]{0,3,1,2:T(8,128)(2,1)S(1)} all-to-all(bf16[128,8,32,64]{0,3,1,2:T(8,128)(2,1)S(1)} %copy.41), channel_id=1, replica_groups=mesh['dp'=8,'ctx'=32] {'ctx'}, dimensions={2} | all-to-all | bytes 8388608 | tf_op jit(solution)/shard_map/all_to_all | solution.py:140
  566.5 4.8 copy.42
  571.3 109.1 %all-gather.9.cloned.1.call-done = bf16[4096,256]{1,0:T(8,128)(2,1)} async-done(((bf16[128,256]{1,0:T(8,128)(2,1)}), bf16[4096,256]{1,0:T(8,128)(2,1)}) %all-gather.9.cloned.1.call-update) | async-done | bytes 2097168 | tf_op jit(solution)/shard_map/all_gather | solution.py:175
  680.4 5.5 fusion.39
  685.9 144.2 %all-gather.7.cloned.1.call-done = bf16[4096,1024]{1,0:T(8,128)(2,1)} async-done(((bf16[128,1024]{1,0:T(8,128)(2,1)}), bf16[4096,1024]{1,0:T(8,128)(2,1)}) %all-gather.7.cloned.1.call-update) | async-done | bytes 8388624 | tf_op jit(solution)/shard_map/all_gather | solution.py:174
  830.1 10.4 %fusion.36 = f32[512,1024]{0,1:T(8,128)S(1)} fusion(bf16[4096,1024]{1,0:T(8,128)(2,1)} %all-gather.7.cloned.1.call-done, bf16[64,8,32,128]{3,2,1,0:T(8,128)(2,1)} %bitcast.126), kind=kOutput, calls=%fused_computation.50 | convolution fusion | flops 4294967296 | bytes 14680064 | tf_op jit(solution)/shard_map/dot_general | solution.py:177
  840.8 2.1 copy.47
  843.0 39.1 %reduce-scatter.7.cloned.1.call-done = f32[64,1280]{1,0:T(8,128)} async-done(((f32[512,1280]{1,0:T(8,128)}), f32[64,1280]{1,0:T(8,128)}) %reduce-scatter.7.cloned.1.call-update) | async-done | bytes 327696 | tf_op jit(solution)/shard_map/reduce_scatter | solution.py:179
  882.1 2.1 multiply_subtract_fusion
  (186 shorter events, 27.1 us)
Async XLA Ops:
  7.2 88.2 %all-gather.11.cloned.1.call-start = ((), (), s32[]{:S(2)}) async-start(), calls=%async_computation.6 | async-start | bytes 1081344 | tf_op jit(solution)/shard_map/all_gather | solution.py:161
  7.9 166.7 %all-gather.13.cloned.1.call-start = ((), (), s32[]{:S(2)}) async-start(), calls=%async_computation.7 | async-start | bytes 1081344 | tf_op jit(solution)/shard_map/all_gather | solution.py:162
  8.6 501.4 %reduce-scatter.5.cloned.1.call-start = ((), (), s32[]{:S(2)}) async-start(), calls=%async_computation.4 | async-start | bytes 4325376 | tf_op jit(solution)/shard_map/reduce_scatter | solution.py:170
  204.6 1.7 copy-start.1
  211.7 1.1 copy-start.2
  212.8 1.7 copy-start.1
  220.2 1.1 copy-start.2
  221.3 1.7 copy-start.1
  228.7 1.1 copy-start.2
  229.8 1.7 copy-start.1
  237.2 1.1 copy-start.2
  238.3 1.7 copy-start.1
  245.7 1.1 copy-start.2
  246.8 1.7 copy-start.1
  254.2 1.1 copy-start.2
  255.3 1.7 copy-start.1
  262.7 1.1 copy-start.2
  263.8 1.7 copy-start.1
  271.1 1.1 copy-start.2
  272.2 239.4 %copy-start = (f32[1024,128]{1,0:T(8,128)S(1)}, f32[1024,128]{1,0:T(8,128)}, u32[]{:S(2)}) copy-start(f32[1024,128]{1,0:T(8,128)} %get-tuple-element.118) | copy-start | bytes 1572868
  272.3 408.1 %all-gather.9.cloned.1.call-start = ((), (), s32[]{:S(2)}) async-start(), calls=%async_computation.5 | async-start | bytes 2162688 | tf_op jit(solution)/shard_map/all_gather | solution.py:175
  511.6 318.5 %all-gather.7.cloned.1.call-start = ((), (), s32[]{:S(2)}) async-start(), calls=%async_computation.3 | async-start | bytes 8650752 | tf_op jit(solution)/shard_map/all_gather | solution.py:174
  512.6 369.5 %reduce-scatter.7.cloned.1.call-start = ((), (), s32[]{:S(2)}) async-start(), calls=%async_computation.8 | async-start | bytes 2949120 | tf_op jit(solution)/shard_map/reduce_scatter | solution.py:179
  842.9 39.1 %copy-start.3 = (f32[64,1280]{1,0:T(8,128)S(1)}, f32[64,1280]{1,0:T(8,128)}, u32[]{:S(2)}) copy-start(f32[64,1280]{1,0:T(8,128)} %param.19) | copy-start | bytes 983044
  842.9 39.1 %copy-start.4 = (f32[64,1280]{1,0:T(8,128)S(1)}, f32[64,1280]{1,0:T(8,128)}, u32[]{:S(2)}) copy-start(f32[64,1280]{1,0:T(8,128)} %param.20) | copy-start | bytes 983044
  843.0 39.1 %copy-start.5 = (f32[64,1280]{1,0:T(8,128)S(1)}, f32[64,1280]{1,0:T(8,128)}, u32[]{:S(2)}) copy-start(f32[64,1280]{1,0:T(8,128)} %param.21) | copy-start | bytes 983044
Sparse Core Ops, SparseCore 0:
  11.4 83.9 all-gather.10
  98.8 75.7 all-gather.12
  272.4 237.6 reduce-scatter.4
  513.9 166.3 all-gather.8
  684.2 145.8 all-gather.6
  843.1 38.9 reduce-scatter.6
where the time goes:
time: 894 us; the launch traced here: 891 us
  waiting for transfers between devices  694 us (78%)
  matrix products  96.5 us (11%)
  blocking collectives  44.4 us (5%)
  local copies, waits for them, and re-layouts  31.2 us (3%)
  between operations  14.2 us (2%)
  other arithmetic  9.15 us (1%)
    reduce_scatter x1, waiting for transfers between devices, per_device(): lax.psum_scatter(key_terms, 'ctx', scatter_dimension=0, tiled=True)  238 us
    all_gather x1, waiting for transfers between devices, per_device(): lax.all_gather(dq_local, 'ctx', axis=0, tiled=True)  144 us
    all_gather x1, waiting for transfers between devices, per_device(): lax.all_gather(kv_mine, 'ctx', axis=0, tiled=True)  109 us
    all_gather x1, waiting for transfers between devices, per_device(): lax.all_gather(keys_here, 'ctx', axis=0, tiled=True)  83.3 us
    all_gather x1, waiting for transfers between devices, per_device(): lax.all_gather(values_here, 'ctx', axis=0, tiled=True)  79.2 us
    all_to_all x1, blocking collectives, per_device(): lax.all_to_all(pieces, 'ctx', split_axis=2, concat_axis=0, tiled=True)  44.4 us
    reduce_scatter x1, waiting for transfers between devices, per_device(): lax.psum_scatter(jnp.concatenate([query_part, key_part], axis=1), 'dp', s...  39.1 us
    dot_general x8, matrix products, backward_advance(): jnp.dot(dscore, key_blk, preferred_element_type=jnp.float32)  18.9 us
  transfers between devices with their start and end apart: 6, of which 6 were waited for; matrix products, arithmetic and copies ran while one was open for 3% of the time, Pallas kernels for 0%

commit v1 on v0

v1 whole, which is shorter than its diff:
```python
import functools
import math

import jax
import jax.numpy as jnp
from jax import lax
from jax.experimental import pallas as pl
from jax.experimental.pallas import tpu as pltpu
from jax.sharding import PartitionSpec as P

STEP = 10
NEG_FILL = -1e30
BETA_ONE = 0.9
BETA_TWO = 0.95
EPSILON = 1e-08
LEARN_RATE = 0.01
DECAY = 0.1

F32 = jnp.float32
BF16 = jnp.bfloat16
MESH = pl.DeviceIdType.MESH
ROW_CONTRACT = (((1,), (1,)), ((), ()))

TOK = 128
HD = 128
HALF = 64
NXY = 16
NCTX = 32
NZ = 8
CHUNK = 256
NCHUNK = 5
KEYS = NCTX * TOK
KT = 512
OWN = 64
ROWS = 1024
SCALE = 1.0 / math.sqrt(HD)


def fused_kernel(
    order_ref,
    x_hbm,
    q_ref,
    k_ref,
    v_ref,
    o_ref,
    grad_ref,
    kv_all,
    k_t,
    x_recv,
    x_t,
    s_scr,
    d_scr,
    dkv_acc,
    dkv_send,
    dkv_recv,
    zkv_send,
    zkv_recv,
    g_all,
    core_send,
    core_recv,
    half_own,
    z_send,
    z_recv,
    kv_ss,
    kv_rs,
    kvz_ss,
    x_ss,
    x_rs,
    g_ss,
    g_rs,
    dkv_ss,
    dkv_rs,
    zkv_ss,
    zkv_rs,
    core_ss,
    core_rs,
    z_ss,
    z_rs,
):
    dp = lax.axis_index("dp")
    ctx = lax.axis_index("ctx")
    core = lax.rem(dp, 2)
    z_lo = dp // 2
    z_hi = lax.rem(ctx, 2)
    plane = ctx // 2
    y = plane // 4
    x = lax.rem(plane, 4)
    z_me = z_hi * 4 + z_lo

    def plane_peer(d):
        return lax.rem(y + d // 4, 4) * 4 + lax.rem(x + lax.rem(d, 4), 4)

    def plane_dev(k):
        return (dp, k * 2 + z_hi)

    def z_peer(d):
        return lax.rem(z_me + d, NZ)

    def z_dev(z):
        return (lax.rem(z, 4) * 2 + core, plane * 2 + z // 4)

    zh_dev = (dp, plane * 2 + (1 - z_hi))
    ctx_other = plane * 2 + (1 - z_hi)
    core_dev = (z_lo * 2 + (1 - core), ctx)

    barrier = pltpu.get_barrier_semaphore()

    @pl.loop(1, NXY)
    def _(d):
        pl.semaphore_signal(barrier, inc=1, device_id=plane_dev(plane_peer(d)), device_id_type=MESH)

    @pl.loop(1, NZ)
    def _(d):
        pl.semaphore_signal(barrier, inc=1, device_id=z_dev(z_peer(d)), device_id_type=MESH)

    pl.semaphore_signal(barrier, inc=1, device_id=core_dev, device_id_type=MESH)

    def rows(first, count):
        return pl.ds(pl.multiple_of(first, count), count)

    my_rows = rows(ctx * TOK, TOK)
    other_rows = rows(ctx_other * TOK, TOK)
    kv_all[my_rows, :HD] = k_ref[...]
    kv_all[my_rows, HD:] = v_ref[...]

    pl.semaphore_wait(barrier, NXY - 1 + NZ - 1 + 1)

    def kv_copy(block_rows, block, d, sems, target):
        return pltpu.make_async_remote_copy(
            src_ref=kv_all.at[block_rows],
            dst_ref=kv_all.at[block_rows],
            send_sem=sems.at[d],
            recv_sem=kv_rs.at[block],
            device_id=target,
            device_id_type=MESH,
        )

    kv_copy(my_rows, ctx, 0, kv_ss, zh_dev).start()

    @pl.loop(1, NXY)
    def _(d):
        kv_copy(my_rows, ctx, d, kv_ss, plane_dev(plane_peer(d))).start()

    kv_copy(other_rows, ctx_other, 0, kv_ss, zh_dev).wait_recv()

    @pl.loop(1, NXY)
    def _(d):
        kv_copy(other_rows, ctx_other, d, kvz_ss, plane_dev(plane_peer(d))).start()

    @pl.loop(1, NXY)
    def _(d):
        k = plane_peer(d)
        for half in range(2):
            block = k * 2 + half
            kv_copy(rows(block * TOK, TOK), block, d, kv_ss, zh_dev).wait_recv()

    def x_copy(k, j, d):
        column = ((j % 4) * 2 + j // 4) * (NCTX * OWN) + k * TOK
        return pltpu.make_async_remote_copy(
            src_ref=x_hbm.at[:, rows(column, TOK)],
            dst_ref=x_recv.at[plane, j],
            send_sem=x_ss.at[d],
            recv_sem=x_rs.at[plane],
            device_id=plane_dev(k),
            device_id_type=MESH,
        )

    def x_own(j):
        column = ((j % 4) * 2 + j // 4) * (NCTX * OWN) + plane * TOK
        return pltpu.make_async_copy(
            x_hbm.at[:, rows(column, TOK)], x_recv.at[plane, j], x_rs.at[plane]
        )

    @pl.loop(1, NXY)
    def _(d):
        for j in range(8):
            x_copy(plane_peer(d), j, d).start()

    for j in range(8):
        x_own(j).start()

    lane = lax.broadcasted_iota(jnp.int32, (1, CHUNK), 1)
    token = lax.rem(lane, TOK)
    query_pos = (
        jnp.where(token < HALF, order_ref[2 * ctx], order_ref[2 * ctx + 1]) * HALF
        + lax.rem(token, HALF)
    )
    sub = lax.broadcasted_iota(jnp.int32, (HALF, CHUNK), 0)

    @pl.loop(0, NCTX)
    def _(b):
        k_t[:, rows(b * TOK, TOK)] = kv_all[rows(b * TOK, TOK), :HD].T

    def g_copy(chunk, k, d):
        piece = g_all.at[chunk, rows(plane * TOK, TOK)]
        return pltpu.make_async_remote_copy(
            src_ref=piece,
            dst_ref=piece,
            send_sem=g_ss.at[chunk, d],
            recv_sem=g_rs.at[chunk, plane],
            device_id=plane_dev(k),
            device_id_type=MESH,
        )

    def send_chunk(chunk):
        @pl.loop(1, NXY)
        def _(d):
            g_copy(chunk, plane_peer(d), d).start()

    def fold(a, op):
        return op(a.reshape(a.shape[0] // 8, 8, a.shape[1]), axis=0)

    for c in range(4):
        heads = (2 * c, 2 * c + 1)
        q_c = jnp.concatenate([q_ref[:, h * HD : (h + 1) * HD] for h in heads], axis=0)
        o_c = jnp.concatenate([o_ref[:, h * HD : (h + 1) * HD] for h in heads], axis=0)

        def scores_tile(t, top):
            first = pl.multiple_of(t * KT, KT)
            s = lax.dot_general(
                kv_all[pl.ds(first, KT), :HD], q_c, ROW_CONTRACT, preferred_element_type=F32
            )
            d_scr[pl.ds(first, KT)] = lax.dot_general(
                kv_all[pl.ds(first, KT), HD:], o_c, ROW_CONTRACT, preferred_element_type=F32
            )
            for b in range(KT // HALF):
                limit = query_pos - order_ref[t * (KT // HALF) + b] * HALF
                part = jnp.where(sub <= limit, s[b * HALF : (b + 1) * HALF], NEG_FILL)
                s_scr[pl.ds(first + b * HALF, HALF)] = part
                top = jnp.maximum(top, fold(part, jnp.max))
            return top

        top = lax.fori_loop(0, KEYS // KT, scores_tile, jnp.full((8, CHUNK), NEG_FILL, F32))
        top = jnp.max(top, axis=0, keepdims=True)

        def weights_tile(t, carried):
            total, inner = carried
            tile = pl.ds(pl.multiple_of(t * KT, KT), KT)
            e = jnp.exp2((s_scr[tile] - top) * (SCALE * math.log2(math.e)))
            s_scr[tile] = e
            return total + fold(e, jnp.sum), inner + fold(e * d_scr[tile], jnp.sum)

        zero = jnp.zeros((8, CHUNK), F32)
        total, inner = lax.fori_loop(0, KEYS // KT, weights_tile, (zero, zero))
        inv = 1.0 / jnp.sum(total, axis=0, keepdims=True)
        delta = jnp.sum(inner, axis=0, keepdims=True) * inv

        def grads_tile(t, dq):
            first = pl.multiple_of(t * KT, KT)
            tile = pl.ds(first, KT)
            p = s_scr[tile] * inv
            ds = (p * (d_scr[tile] - delta) * SCALE).astype(BF16)
            dk = jnp.dot(ds, q_c, preferred_element_type=F32)
            dv = jnp.dot(p.astype(BF16), o_c, preferred_element_type=F32)
            if c == 0:
                dkv_acc[tile, :HD] = dk
                dkv_acc[tile, HD:] = dv
            elif c < 3:
                dkv_acc[tile, :HD] += dk
                dkv_acc[tile, HD:] += dv
            else:
                dkv_send[tile, :HD] = (dkv_acc[tile, :HD] + dk).astype(BF16)
                dkv_send[tile, HD:] = (dkv_acc[tile, HD:] + dv).astype(BF16)
            return dq + jnp.dot(k_t[:, tile], ds, preferred_element_type=F32)

        dq = lax.fori_loop(0, KEYS // KT, grads_tile, jnp.zeros((HD, CHUNK), F32))
        for i in range(2):
            g_all[c, rows(plane * TOK, TOK), i * HD : (i + 1) * HD] = (
                dq[:, i * TOK : (i + 1) * TOK].T.astype(BF16)
            )
        if c == 3:
            @pl.loop(1, NXY)
            def _(d):
                dkv_copy(dkv_send, dkv_recv, dkv_ss, dkv_rs, plane, plane_peer(d), d, plane_dev).start()
        send_chunk(c)

    for j in range(8):
        x_own(j).wait()

    def transpose_slot(k):
        for j in range(8):
            x_t[j * TOK : (j + 1) * TOK, rows(k * TOK, TOK)] = x_recv[k, j].T

    transpose_slot(plane)

    @pl.loop(1, NXY)
    def _(d):
        k = plane_peer(d)
        pltpu.make_async_copy(x_recv.at[k], x_recv.at[k], x_rs.at[k]).wait()
        transpose_slot(k)

    def sum_slot(d, total):
        k = plane_peer(d)
        dkv_copy(dkv_send, dkv_recv, dkv_ss, dkv_rs, k, plane, d, plane_dev).wait_recv()
        return total + dkv_recv[k].astype(F32)

    half_own_kv = lax.fori_loop(
        1, NXY, sum_slot, dkv_send[rows(plane * 2 * TOK, 2 * TOK)].astype(F32)
    )
    zkv_send[...] = half_own_kv.astype(BF16)
    zkv = pltpu.make_async_remote_copy(
        src_ref=zkv_send.at[rows((1 - z_hi) * TOK, TOK)],
        dst_ref=zkv_recv,
        send_sem=zkv_ss,
        recv_sem=zkv_rs,
        device_id=zh_dev,
        device_id_type=MESH,
    )
    zkv.start()
    own_kv = jnp.where(z_hi == 0, half_own_kv[:TOK], half_own_kv[TOK:])
    zkv.wait_recv()
    g_all[4, rows(plane * TOK, TOK)] = (own_kv + zkv_recv[...].astype(F32)).astype(BF16)
    send_chunk(4)

    def z_copy(chunk, z, d):
        return pltpu.make_async_remote_copy(
            src_ref=z_send.at[chunk, z],
            dst_ref=z_recv.at[chunk, z_me],
            send_sem=z_ss.at[chunk, d],
            recv_sem=z_rs.at[chunk, z_me],
            device_id=z_dev(z),
            device_id_type=MESH,
        )

    def z_arrived(chunk, z):
        return pltpu.make_async_remote_copy(
            src_ref=z_send.at[chunk, z],
            dst_ref=z_recv.at[chunk, z],
            send_sem=z_ss.at[chunk, 0],
            recv_sem=z_rs.at[chunk, z],
            device_id=z_dev(z),
            device_id_type=MESH,
        )

    def core_copy(chunk):
        return pltpu.make_async_remote_copy(
            src_ref=core_send.at[chunk],
            dst_ref=core_recv.at[chunk],
            send_sem=core_ss.at[chunk],
            recv_sem=core_rs.at[chunk],
            device_id=core_dev,
            device_id_type=MESH,
        )

    for c in range(NCHUNK):
        @pl.loop(1, NXY)
        def _(d):
            k = plane_peer(d)
            piece = g_all.at[c, rows(k * TOK, TOK)]
            pltpu.make_async_remote_copy(
                src_ref=piece,
                dst_ref=piece,
                send_sem=g_ss.at[c, d],
                recv_sem=g_rs.at[c, k],
                device_id=plane_dev(k),
                device_id_type=MESH,
            ).wait_recv()

        def product(first):
            return jnp.dot(
                x_t[pl.ds(pl.multiple_of(first, 256), 256)], g_all[c], preferred_element_type=F32
            )

        @pl.loop(0, 2)
        def _(i):
            core_send[c, rows(i * 256, 256)] = product((1 - core) * 512 + i * 256)

        core_copy(c).start()

        @pl.loop(0, 2)
        def _(i):
            half_own[c, rows(i * 256, 256)] = product(core * 512 + i * 256)

        core_copy(c).wait_recv()
        for j in range(NZ):
            z = (j % 2) * 4 + j // 2
            part = pl.ds(j * OWN, OWN)
            total = half_own[c, part] + core_recv[c, part]
            half_own[c, part] = total
            z_send[c, z] = total.astype(BF16)

        @pl.loop(1, NZ)
        def _(d):
            z_copy(c, z_peer(d), d).start()

    for c in range(NCHUNK):
        def add_slot(d, total):
            z = z_peer(d)
            z_arrived(c, z).wait_recv()
            return total + z_recv[c, z].astype(F32)

        own_part = half_own[c, rows((z_lo * 2 + z_hi) * OWN, OWN)]
        grad_ref[:, c * CHUNK : (c + 1) * CHUNK] = lax.fori_loop(1, NZ, add_slot, own_part)

    kv_copy(my_rows, ctx, 0, kv_ss, zh_dev).wait_send()
    zkv.wait_send()

    @pl.loop(1, NXY)
    def _(d):
        k = plane_peer(d)
        kv_copy(my_rows, ctx, d, kv_ss, plane_dev(k)).wait_send()
        kv_copy(other_rows, ctx_other, d, kvz_ss, plane_dev(k)).wait_send()
        pltpu.make_async_copy(x_recv.at[k], x_recv.at[k], x_ss.at[d]).wait()
        dkv_copy(dkv_send, dkv_recv, dkv_ss, dkv_rs, plane, k, d, plane_dev).wait_send()
        for c in range(NCHUNK):
            g_copy(c, k, d).wait_send()

    for c in range(NCHUNK):
        core_copy(c).wait_send()

        @pl.loop(1, NZ)
        def _(d):
            z_copy(c, z_peer(d), d).wait_send()


def dkv_copy(send, recv, ss, rs, source, k, d, plane_dev):
    return pltpu.make_async_remote_copy(
        src_ref=send.at[pl.ds(pl.multiple_of(k * 2 * TOK, 2 * TOK), 2 * TOK)],
        dst_ref=recv.at[source],
        send_sem=ss.at[d],
        recv_sem=rs.at[source],
        device_id=plane_dev(k),
        device_id_type=MESH,
    )


def fused(order, x, q, k, v, o):
    vmem = pl.BlockSpec(memory_space=pltpu.VMEM)
    dma = pltpu.SemaphoreType.DMA
    scratch = [
        pltpu.VMEM((KEYS, 2 * HD), BF16),
        pltpu.VMEM((HD, KEYS), BF16),
        pltpu.VMEM((NXY, 8, TOK, TOK), BF16),
        pltpu.VMEM((ROWS, NXY * TOK), BF16),
        pltpu.VMEM((KEYS, CHUNK), F32),
        pltpu.VMEM((KEYS, CHUNK), F32),
        pltpu.VMEM((KEYS, 2 * HD), F32),
        pltpu.VMEM((KEYS, 2 * HD), BF16),
        pltpu.VMEM((NXY, 2 * TOK, 2 * HD), BF16),
        pltpu.VMEM((2 * TOK, 2 * HD), BF16),
        pltpu.VMEM((TOK, 2 * HD), BF16),
        pltpu.VMEM((NCHUNK, NXY * TOK, CHUNK), BF16),
        pltpu.VMEM((NCHUNK, ROWS // 2, CHUNK), F32),
        pltpu.VMEM((NCHUNK, ROWS // 2, CHUNK), F32),
        pltpu.VMEM((NCHUNK, ROWS // 2, CHUNK), F32),
        pltpu.VMEM((NCHUNK, NZ, OWN, CHUNK), BF16),
        pltpu.VMEM((NCHUNK, NZ, OWN, CHUNK), BF16),
        dma((NXY,)),
        dma((NCTX,)),
        dma((NXY,)),
        dma((NXY,)),
        dma((NXY,)),
        dma((NCHUNK, NXY)),
        dma((NCHUNK, NXY)),
        dma((NXY,)),
        dma((NXY,)),
        dma,
        dma,
        dma((NCHUNK,)),
        dma((NCHUNK,)),
        dma((NCHUNK, NZ)),
        dma((NCHUNK, NZ)),
    ]
    return pl.pallas_call(
        fused_kernel,
        name="attention_backward_and_weight_gradient",
        out_shape=jax.ShapeDtypeStruct((OWN, NCHUNK * CHUNK), F32),
        in_specs=[
            pl.BlockSpec(memory_space=pltpu.SMEM),
            pl.BlockSpec(memory_space=pl.ANY),
            vmem,
            vmem,
            vmem,
            vmem,
        ],
        out_specs=vmem,
        scratch_shapes=scratch,
        compiler_params=pltpu.CompilerParams(
            collective_id=0, has_side_effects=True, vmem_limit_bytes=60 * 2**20
        ),
    )(order, x, q, k, v, o)


def per_device(
    layer_input,
    query_rows,
    key_rows,
    value_rows,
    out_grad,
    block_order,
    master,
    moment_one,
    moment_two,
):
    grad_local = fused(
        block_order, layer_input[0], query_rows[0], key_rows[0], value_rows[0], out_grad[0]
    )
    new_one = BETA_ONE * moment_one + (1.0 - BETA_ONE) * grad_local
    new_two = BETA_TWO * moment_two + (1.0 - BETA_TWO) * grad_local * grad_local
    corr_one = 1.0 - BETA_ONE**STEP
    corr_two = 1.0 - BETA_TWO**STEP
    update = new_one / corr_one / (jnp.sqrt(new_two / corr_two) + EPSILON)
    new_master = master - LEARN_RATE * (update + DECAY * master)
    return (new_master, new_one, new_two)


def solution(mesh):
    rows = P("dp", "ctx", None)
    owned = P(("dp", "ctx"), None)
    return jax.shard_map(
        per_device,
        mesh=mesh,
        in_specs=(rows, rows, rows, rows, rows, P(), owned, owned, owned),
        out_specs=(owned, owned, owned),
        check_vma=False,
    )
```

time: 894 us -> 209 us (0.23)
  waiting for transfers between devices: 694 us -> 0 us
  Pallas kernels: 0 us -> 206 us
  matrix products: 96.5 us -> 0 us
  blocking collectives: 44.4 us -> 0 us
  local copies, waits for them, and re-layouts: 31.2 us -> 0.01 us
  between operations: 14.2 us -> 0.69 us
    all_gather x4 -> x0, waiting for transfers between devices: 416 us -> none  [the longest x1 144 us: per_device(): lax.all_gather(dq_local, 'ctx', axis=0, tiled=True)]
    reduce_scatter x2 -> x0, waiting for transfers between devices: 277 us -> none  [the longest x1 238 us: per_device(): lax.psum_scatter(key_terms, 'ctx', scatter_dimension=0, tiled=True)]
    pallas_call x0 -> x1, Pallas kernels: none -> 206 us  [fused(): pl.pallas_call(fused_kernel, name='attention_backward_and_weight_gradient...]
    dot_general x58 -> x0, matrix products: 96.5 us -> none  [the longest x8 18.9 us: backward_advance(): jnp.dot(dscore, key_blk, preferred_element_type=jnp.float32)]
    all_to_all x1 -> x0, blocking collectives: 44.4 us -> none  [per_device(): lax.all_to_all(pieces, 'ctx', split_axis=2, concat_axis=0, tiled=True)]
  transfers between devices with their start and end apart: 6 -> 0, of which waited for: 6 -> 0; matrix products, arithmetic and copies ran while one was open for 3% -> 0% of each run, Pallas kernels for 0% -> 0%
where the time goes in v1:
time: 209 us; the launch traced here: 208 us
  Pallas kernels  206 us (99%)
    pallas_call x1, Pallas kernels, fused(): pl.pallas_call(fused_kernel, name='attention_backward_and_weight_gradient...  206 us

profile of v1, /device:TPU:1, one launch (start us, length us, event | category | flops | bytes accessed | tf_op | source)
XLA Modules:
  0.0 208.5 jit_solution(5399536337614050541)
XLA Ops:
  0.6 0.0 copy-start.2
  0.6 0.0 copy-start.1
  0.7 0.0 copy-start
  0.7 205.7 %attention_backward_and_weight_gradient.1 = f32[64,1280]{1,0:T(8,128)} custom-call(s32[64]{0:T(128)} %order_ref.1, bf16[128,16384]{1,0:T(8,128)(2,1)} %bitcast.5, bf16[128,1024]{1,0:T(8,128)(2,1)} %bitcast.6, bf16[128,128]{1,0:T(8,128)(2,1)} %bitcast.8, bf16[128,128]{1,0:T(8,128)(2,1)} %bitcast.9, bf16[128,1024]{1,0:T(8,128)(2,1)} %bitcast.7), custom_call_target="tpu_custom_call" | custom-call | tf_op jit(solution)/shard_map/attention_backward_and_weight_gradient/pallas_call | solution.py:464
  206.4 0.0 copy-done.2
  206.4 0.0 copy-done.1
  206.4 0.0 copy-done
  206.4 2.1 multiply_subtract_fusion
Async XLA Ops:
  0.6 205.7 %copy-start.2 = (f32[64,1280]{1,0:T(8,128)S(1)}, f32[64,1280]{1,0:T(8,128)}, u32[]{:S(2)}) copy-start(f32[64,1280]{1,0:T(8,128)} %param.17) | copy-start | bytes 983044
  0.6 205.7 %copy-start.1 = (f32[64,1280]{1,0:T(8,128)S(1)}, f32[64,1280]{1,0:T(8,128)}, u32[]{:S(2)}) copy-start(f32[64,1280]{1,0:T(8,128)} %param.16) | copy-start | bytes 983044
  0.7 205.7 %copy-start = (f32[64,1280]{1,0:T(8,128)S(1)}, f32[64,1280]{1,0:T(8,128)}, u32[]{:S(2)}) copy-start(f32[64,1280]{1,0:T(8,128)} %param.15) | copy-start | bytes 983044

commit v2 on v1

--- a/solution.py
+++ b/solution.py
@@ -52,7 +52,9 @@
     d_scr,
     dkv_acc,
     dkv_send,
-    dkv_recv,
+    dkv_one,
+    dkv_sum,
+    dkv_two,
     zkv_send,
     zkv_recv,
     g_all,
@@ -61,15 +63,22 @@
     half_own,
     z_send,
     z_recv,
-    kv_ss,
-    kv_rs,
     kvz_ss,
+    kvz_rs,
+    kv1_ss,
+    kv1_rs,
+    kv2_ss,
+    kv2_rs,
     x_ss,
     x_rs,
-    g_ss,
-    g_rs,
-    dkv_ss,
-    dkv_rs,
+    g1_ss,
+    g1_rs,
+    g2_ss,
+    g2_rs,
+    dkv1_ss,
+    dkv1_rs,
+    dkv2_ss,
+    dkv2_rs,
     zkv_ss,
     zkv_rs,
     core_ss,
@@ -100,7 +109,27 @@
         return (lax.rem(z, 4) * 2 + core, plane * 2 + z // 4)
 
     zh_dev = (dp, plane * 2 + (1 - z_hi))
-    ctx_other = plane * 2 + (1 - z_hi)
+    place = (y, x)
+
+    def line_dev(axis, i):
+        return plane_dev(i * 4 + x if axis == 0 else y * 4 + i)
+
+    def line_peer(axis, d):
+        return lax.rem(place[axis] + d, 4)
+
+    def remote(src, dst, ss, rs, target):
+        return pltpu.make_async_remote_copy(
+            src_ref=src,
+            dst_ref=dst,
+            send_sem=ss,
+            recv_sem=rs,
+            device_id=target,
+            device_id_type=MESH,
+        )
+
+    def across(array, half, i):
+        return array.at[half, :, i] if half == 0 else array.at[half, i]
+
     core_dev = (z_lo * 2 + (1 - core), ctx)
 
     barrier = pltpu.get_barrier_semaphore()
@@ -118,41 +147,70 @@
     def rows(first, count):
         return pl.ds(pl.multiple_of(first, count), count)
 
-    my_rows = rows(ctx * TOK, TOK)
-    other_rows = rows(ctx_other * TOK, TOK)
-    kv_all[my_rows, :HD] = k_ref[...]
-    kv_all[my_rows, HD:] = v_ref[...]
+    kv_all[0, y, x, z_hi] = k_ref[...]
+    kv_all[1, y, x, z_hi] = v_ref[...]
 
     pl.semaphore_wait(barrier, NXY - 1 + NZ - 1 + 1)
 
-    def kv_copy(block_rows, block, d, sems, target):
-        return pltpu.make_async_remote_copy(
-            src_ref=kv_all.at[block_rows],
-            dst_ref=kv_all.at[block_rows],
-            send_sem=sems.at[d],
-            recv_sem=kv_rs.at[block],
-            device_id=target,
-            device_id_type=MESH,
-        )
-
-    kv_copy(my_rows, ctx, 0, kv_ss, zh_dev).start()
-
-    @pl.loop(1, NXY)
-    def _(d):
-        kv_copy(my_rows, ctx, d, kv_ss, plane_dev(plane_peer(d))).start()
-
-    kv_copy(other_rows, ctx_other, 0, kv_ss, zh_dev).wait_recv()
-
-    @pl.loop(1, NXY)
-    def _(d):
-        kv_copy(other_rows, ctx_other, d, kvz_ss, plane_dev(plane_peer(d))).start()
-
-    @pl.loop(1, NXY)
-    def _(d):
-        k = plane_peer(d)
-        for half in range(2):
-            block = k * 2 + half
-            kv_copy(rows(block * TOK, TOK), block, d, kv_ss, zh_dev).wait_recv()
+    kvz = remote(
+        kv_all.at[:, y, x, z_hi], kv_all.at[:, y, x, z_hi], kvz_ss, kvz_rs, zh_dev
+    )
+
+    def kv_one(z, half, d):
+        piece = kv_all.at[half, y, x, z]
+        return remote(
+            piece,
+            piece,
+            kv1_ss.at[z, half, d],
+            kv1_rs.at[z, half, place[half]],
+            line_dev(half, line_peer(half, d)),
+        )
+
+    def kv_one_arrived(z, half, d):
+        i = line_peer(half, d)
+        piece = kv_all.at[half, i, x, z] if half == 0 else kv_all.at[half, y, i, z]
+        return remote(
+            piece, piece, kv1_ss.at[z, half, d], kv1_rs.at[z, half, i], line_dev(half, i)
+        )
+
+    def kv_line(z, half, i):
+        return kv_all.at[half, :, i, z] if half == 0 else kv_all.at[half, i, :, z]
+
+    def kv_two(z, half, d):
+        axis = 1 - half
+        piece = kv_line(z, half, place[axis])
+        return remote(
+            piece,
+            piece,
+            kv2_ss.at[z, half, d],
+            kv2_rs.at[z, half, place[axis]],
+            line_dev(axis, line_peer(axis, d)),
+        )
+
+    def kv_two_arrived(z, half, d):
+        axis = 1 - half
+        i = line_peer(axis, d)
+        piece = kv_line(z, half, i)
+        return remote(
+            piece, piece, kv2_ss.at[z, half, d], kv2_rs.at[z, half, i], line_dev(axis, i)
+        )
+
+    steps = [(half, d) for d in (1, 3, 2) for half in (0, 1)]
+    kvz.start()
+    for half, d in steps:
+        kv_one(z_hi, half, d).start()
+    kvz.wait_recv()
+    for half, d in steps:
+        kv_one(1 - z_hi, half, d).start()
+    for z in (z_hi, 1 - z_hi):
+        for half in (0, 1):
+            for d in (1, 3, 2):
+                kv_one_arrived(z, half, d).wait_recv()
+            for d in (1, 3, 2):
+                kv_two(z, half, d).start()
+    for z in (z_hi, 1 - z_hi):
+        for half, d in steps:
+            kv_two_arrived(z, half, d).wait_recv()
 
     def x_copy(k, j, d):
         column = ((j % 4) * 2 + j // 4) * (NCTX * OWN) + k * TOK
@@ -189,23 +247,99 @@
 
     @pl.loop(0, NCTX)
     def _(b):
-        k_t[:, rows(b * TOK, TOK)] = kv_all[rows(b * TOK, TOK), :HD].T
-
-    def g_copy(chunk, k, d):
-        piece = g_all.at[chunk, rows(plane * TOK, TOK)]
-        return pltpu.make_async_remote_copy(
-            src_ref=piece,
-            dst_ref=piece,
-            send_sem=g_ss.at[chunk, d],
-            recv_sem=g_rs.at[chunk, plane],
-            device_id=plane_dev(k),
-            device_id_type=MESH,
+        k_t[:, rows(b * TOK, TOK)] = kv_all[0, b // 8, lax.rem(b // 2, 4), lax.rem(b, 2)].T
+
+    def g_one(chunk, half, d):
+        piece = g_all.at[chunk, half, y, x]
+        return remote(
+            piece,
+            piece,
+            g1_ss.at[chunk, half, d],
+            g1_rs.at[chunk, half, place[half]],
+            line_dev(half, line_peer(half, d)),
+        )
+
+    def g_one_arrived(chunk, half, d):
+        i = line_peer(half, d)
+        piece = g_all.at[chunk, half, i, x] if half == 0 else g_all.at[chunk, half, y, i]
+        return remote(
+            piece, piece, g1_ss.at[chunk, half, d], g1_rs.at[chunk, half, i], line_dev(half, i)
+        )
+
+    def g_two(chunk, half, d):
+        axis = 1 - half
+        piece = across(g_all.at[chunk], half, place[axis])
+        return remote(
+            piece,
+            piece,
+            g2_ss.at[chunk, half, d],
+            g2_rs.at[chunk, half, place[axis]],
+            line_dev(axis, line_peer(axis, d)),
+        )
+
+    def g_two_arrived(chunk, half, d):
+        axis = 1 - half
+        i = line_peer(axis, d)
+        piece = across(g_all.at[chunk], half, i)
+        return remote(
+            piece, piece, g2_ss.at[chunk, half, d], g2_rs.at[chunk, half, i], line_dev(axis, i)
         )
 
     def send_chunk(chunk):
-        @pl.loop(1, NXY)
-        def _(d):
-            g_copy(chunk, plane_peer(d), d).start()
+        for half, d in steps:
+            g_one(chunk, half, d).start()
+
+    def forward_chunk(chunk):
+        for half in (0, 1):
+            for d in (1, 3, 2):
+                g_one_arrived(chunk, half, d).wait_recv()
+            for d in (1, 3, 2):
+                g_two(chunk, half, d).start()
+
+    def dkv_first(half, d):
+        i = line_peer(half, d)
+        return remote(
+            dkv_send.at[half, i] if half == 0 else dkv_send.at[half, :, i],
+            dkv_one.at[half, place[half]],
+            dkv1_ss.at[half, d],
+            dkv1_rs.at[half, place[half]],
+            line_dev(half, i),
+        )
+
+    def dkv_first_arrived(half, d):
+        i = line_peer(half, d)
+        return remote(
+            dkv_one.at[half, i],
+            dkv_one.at[half, i],
+            dkv1_ss.at[half, d],
+            dkv1_rs.at[half, i],
+            line_dev(half, i),
+        )
+
+    def dkv_second(half, d):
+        axis = 1 - half
+        i = line_peer(axis, d)
+        return remote(
+            dkv_sum.at[half, i],
+            dkv_two.at[half, place[axis]],
+            dkv2_ss.at[half, d],
+            dkv2_rs.at[half, place[axis]],
+            line_dev(axis, i),
+        )
+
+    def dkv_second_arrived(half, d):
+        axis = 1 - half
+        i = line_peer(axis, d)
+        return remote(
+            dkv_two.at[half, i],
+            dkv_two.at[half, i],
+            dkv2_ss.at[half, d],
+            dkv2_rs.at[half, i],
+            line_dev(axis, i),
+        )
+
+    def key_tile(ref, half, t):
+        return ref.at[half, t // 2, pl.ds(lax.rem(t, 2) * 2, 2)]
 
     def fold(a, op):
         return op(a.reshape(a.shape[0] // 8, 8, a.shape[1]), axis=0)
@@ -218,10 +352,10 @@
         def scores_tile(t, top):
             first = pl.multiple_of(t * KT, KT)
             s = lax.dot_general(
-                kv_all[pl.ds(first, KT), :HD], q_c, ROW_CONTRACT, preferred_element_type=F32
+                key_tile(kv_all, 0, t)[...].reshape(KT, HD), q_c, ROW_CONTRACT, preferred_element_type=F32
             )
             d_scr[pl.ds(first, KT)] = lax.dot_general(
-                kv_all[pl.ds(first, KT), HD:], o_c, ROW_CONTRACT, preferred_element_type=F32
+                key_tile(kv_all, 1, t)[...].reshape(KT, HD), o_c, ROW_CONTRACT, preferred_element_type=F32
             )
             for b in range(KT // HALF):
                 limit = query_pos - order_ref[t * (KT // HALF) + b] * HALF
@@ -259,20 +393,51 @@
                 dkv_acc[tile, :HD] += dk
                 dkv_acc[tile, HD:] += dv
             else:
-                dkv_send[tile, :HD] = (dkv_acc[tile, :HD] + dk).astype(BF16)
-                dkv_send[tile, HD:] = (dkv_acc[tile, HD:] + dv).astype(BF16)
+                dk = (dkv_acc[tile, :HD] + dk).astype(BF16)
+                dv = (dkv_acc[tile, HD:] + dv).astype(BF16)
+                key_tile(dkv_send, 0, t)[...] = dk.reshape(2, 2, TOK, HD)
+                key_tile(dkv_send, 1, t)[...] = dv.reshape(2, 2, TOK, HD)
             return dq + jnp.dot(k_t[:, tile], ds, preferred_element_type=F32)
 
         dq = lax.fori_loop(0, KEYS // KT, grads_tile, jnp.zeros((HD, CHUNK), F32))
         for i in range(2):
-            g_all[c, rows(plane * TOK, TOK), i * HD : (i + 1) * HD] = (
-                dq[:, i * TOK : (i + 1) * TOK].T.astype(BF16)
-            )
+            g_all[c, i, y, x] = dq[:, i * TOK : (i + 1) * TOK].T.astype(BF16)
         if c == 3:
-            @pl.loop(1, NXY)
-            def _(d):
-                dkv_copy(dkv_send, dkv_recv, dkv_ss, dkv_rs, plane, plane_peer(d), d, plane_dev).start()
+            for half, d in steps:
+                dkv_first(half, d).start()
         send_chunk(c)
+        if c > 0:
+            forward_chunk(c - 1)
+
+    for half in (0, 1):
+        for d in (1, 3, 2):
+            dkv_first_arrived(half, d).wait_recv()
+        for j in range(4):
+            piece = dkv_send[half, y, j] if half == 0 else dkv_send[half, j, x]
+            total = piece.astype(F32)
+            for d in (1, 3, 2):
+                total += dkv_one[half, line_peer(half, d), j].astype(F32)
+            dkv_sum[half, j] = total
+        for d in (1, 3, 2):
+            dkv_second(half, d).start()
+
+    forward_chunk(3)
+
+    for half in (0, 1):
+        axis = 1 - half
+        total = dkv_sum[half, place[axis]]
+        for d in (1, 3, 2):
+            dkv_second_arrived(half, d).wait_recv()
+            total += dkv_two[half, line_peer(axis, d)]
+        zkv_send[0, half] = total[0]
+        zkv_send[1, half] = total[1]
+    zkv = remote(zkv_send.at[1 - z_hi], zkv_recv, zkv_ss, zkv_rs, zh_dev)
+    zkv.start()
+    zkv.wait_recv()
+    for half in (0, 1):
+        g_all[4, half, y, x] = (zkv_send[z_hi, half] + zkv_recv[half]).astype(BF16)
+    send_chunk(4)
+    forward_chunk(4)
 
     for j in range(8):
         x_own(j).wait()
@@ -288,29 +453,6 @@
         k = plane_peer(d)
         pltpu.make_async_copy(x_recv.at[k], x_recv.at[k], x_rs.at[k]).wait()
         transpose_slot(k)
-
-    def sum_slot(d, total):
-        k = plane_peer(d)
-        dkv_copy(dkv_send, dkv_recv, dkv_ss, dkv_rs, k, plane, d, plane_dev).wait_recv()
-        return total + dkv_recv[k].astype(F32)
-
-    half_own_kv = lax.fori_loop(
-        1, NXY, sum_slot, dkv_send[rows(plane * 2 * TOK, 2 * TOK)].astype(F32)
-    )
-    zkv_send[...] = half_own_kv.astype(BF16)
-    zkv = pltpu.make_async_remote_copy(
-        src_ref=zkv_send.at[rows((1 - z_hi) * TOK, TOK)],
-        dst_ref=zkv_recv,
-        send_sem=zkv_ss,
-        recv_sem=zkv_rs,
-        device_id=zh_dev,
-        device_id_type=MESH,
-    )
-    zkv.start()
-    own_kv = jnp.where(z_hi == 0, half_own_kv[:TOK], half_own_kv[TOK:])
-    zkv.wait_recv()
-    g_all[4, rows(plane * TOK, TOK)] = (own_kv + zkv_recv[...].astype(F32)).astype(BF16)
-    send_chunk(4)
 
     def z_copy(chunk, z, d):
         return pltpu.make_async_remote_copy(
@@ -343,22 +485,15 @@
         )
 
     for c in range(NCHUNK):
-        @pl.loop(1, NXY)
-        def _(d):
-            k = plane_peer(d)
-            piece = g_all.at[c, rows(k * TOK, TOK)]
-            pltpu.make_async_remote_copy(
-                src_ref=piece,
-                dst_ref=piece,
-                send_sem=g_ss.at[c, d],
-                recv_sem=g_rs.at[c, k],
-                device_id=plane_dev(k),
-                device_id_type=MESH,
-            ).wait_recv()
+        for half, d in steps:
+            g_two_arrived(c, half, d).wait_recv()
+        columns = jnp.concatenate(
+            [g_all[c, half].reshape(NXY * TOK, HD) for half in (0, 1)], axis=1
+        )
 
         def product(first):
             return jnp.dot(
-                x_t[pl.ds(pl.multiple_of(first, 256), 256)], g_all[c], preferred_element_type=F32
+                x_t[pl.ds(pl.multiple_of(first, 256), 256)], columns, preferred_element_type=F32
             )
 
         @pl.loop(0, 2)
@@ -392,18 +527,22 @@
         own_part = half_own[c, rows((z_lo * 2 + z_hi) * OWN, OWN)]
         grad_ref[:, c * CHUNK : (c + 1) * CHUNK] = lax.fori_loop(1, NZ, add_slot, own_part)
 
-    kv_copy(my_rows, ctx, 0, kv_ss, zh_dev).wait_send()
+    kvz.wait_send()
     zkv.wait_send()
+    for half, d in steps:
+        for z in (z_hi, 1 - z_hi):
+            kv_one(z, half, d).wait_send()
+            kv_two(z, half, d).wait_send()
+        dkv_first(half, d).wait_send()
+        dkv_second(half, d).wait_send()
+        for c in range(NCHUNK):
+            g_one(c, half, d).wait_send()
+            g_two(c, half, d).wait_send()
 
     @pl.loop(1, NXY)
     def _(d):
         k = plane_peer(d)
-        kv_copy(my_rows, ctx, d, kv_ss, plane_dev(k)).wait_send()
-        kv_copy(other_rows, ctx_other, d, kvz_ss, plane_dev(k)).wait_send()
         pltpu.make_async_copy(x_recv.at[k], x_recv.at[k], x_ss.at[d]).wait()
-        dkv_copy(dkv_send, dkv_recv, dkv_ss, dkv_rs, plane, k, d, plane_dev).wait_send()
-        for c in range(NCHUNK):
-            g_copy(c, k, d).wait_send()
 
     for c in range(NCHUNK):
         core_copy(c).wait_send()
@@ -411,49 +550,47 @@
         @pl.loop(1, NZ)
         def _(d):
             z_copy(c, z_peer(d), d).wait_send()
-
-
-def dkv_copy(send, recv, ss, rs, source, k, d, plane_dev):
-    return pltpu.make_async_remote_copy(
-        src_ref=send.at[pl.ds(pl.multiple_of(k * 2 * TOK, 2 * TOK), 2 * TOK)],
-        dst_ref=recv.at[source],
-        send_sem=ss.at[d],
-        recv_sem=rs.at[source],
-        device_id=plane_dev(k),
-        device_id_type=MESH,
-    )
 
 
 def fused(order, x, q, k, v, o):
     vmem = pl.BlockSpec(memory_space=pltpu.VMEM)
     dma = pltpu.SemaphoreType.DMA
     scratch = [
-        pltpu.VMEM((KEYS, 2 * HD), BF16),
+        pltpu.VMEM((2, 4, 4, 2, TOK, HD), BF16),
         pltpu.VMEM((HD, KEYS), BF16),
         pltpu.VMEM((NXY, 8, TOK, TOK), BF16),
         pltpu.VMEM((ROWS, NXY * TOK), BF16),
         pltpu.VMEM((KEYS, CHUNK), F32),
         pltpu.VMEM((KEYS, CHUNK), F32),
         pltpu.VMEM((KEYS, 2 * HD), F32),
-        pltpu.VMEM((KEYS, 2 * HD), BF16),
-        pltpu.VMEM((NXY, 2 * TOK, 2 * HD), BF16),
-        pltpu.VMEM((2 * TOK, 2 * HD), BF16),
-        pltpu.VMEM((TOK, 2 * HD), BF16),
-        pltpu.VMEM((NCHUNK, NXY * TOK, CHUNK), BF16),
+        pltpu.VMEM((2, 4, 4, 2, TOK, HD), BF16),
+        pltpu.VMEM((2, 4, 4, 2, TOK, HD), BF16),
+        pltpu.VMEM((2, 4, 2, TOK, HD), F32),
+        pltpu.VMEM((2, 4, 2, TOK, HD), F32),
+        pltpu.VMEM((2, 2, TOK, HD), F32),
+        pltpu.VMEM((2, TOK, HD), F32),
+        pltpu.VMEM((NCHUNK, 2, 4, 4, TOK, HD), BF16),
         pltpu.VMEM((NCHUNK, ROWS // 2, CHUNK), F32),
         pltpu.VMEM((NCHUNK, ROWS // 2, CHUNK), F32),
         pltpu.VMEM((NCHUNK, ROWS // 2, CHUNK), F32),
         pltpu.VMEM((NCHUNK, NZ, OWN, CHUNK), BF16),
         pltpu.VMEM((NCHUNK, NZ, OWN, CHUNK), BF16),
-        dma((NXY,)),
-        dma((NCTX,)),
+        dma,
+        dma,
+        dma((2, 2, 4)),
+        dma((2, 2, 4)),
+        dma((2, 2, 4)),
+        dma((2, 2, 4)),
         dma((NXY,)),
         dma((NXY,)),
-        dma((NXY,)),
-        dma((NCHUNK, NXY)),
-        dma((NCHUNK, NXY)),
-        dma((NXY,)),
-        dma((NXY,)),
+        dma((NCHUNK, 2, 4)),
+        dma((NCHUNK, 2, 4)),
+        dma((NCHUNK, 2, 4)),
+        dma((NCHUNK, 2, 4)),
+        dma((2, 4)),
+        dma((2, 4)),
+        dma((2, 4)),
+        dma((2, 4)),
         dma,
         dma,
         dma((NCHUNK,)),

time: 209 us -> 194 us (0.928)
  Pallas kernels: 206 us -> 191 us
    pallas_call x1, Pallas kernels: 206 us -> 191 us  [fused(): pl.pallas_call(fused_kernel, name='attention_backward_and_weight_gradient...]
where the time goes in v2:
time: 194 us
  Pallas kernels  191 us (98%)
  other arithmetic  2.06 us (1%)
    pallas_call x1, Pallas kernels, fused(): pl.pallas_call(fused_kernel, name='attention_backward_and_weight_gradient...  191 us

profile of v2, /device:TPU:1, one launch (start us, length us, event | category | flops | bytes accessed | tf_op | source)
XLA Modules:
  0.0 193.7 jit_solution(10518387255955813781)
XLA Ops:
  0.6 0.0 copy-start.2
  0.6 0.0 copy-start.1
  0.7 0.0 copy-start
  0.7 191.0 %attention_backward_and_weight_gradient.1 = f32[64,1280]{1,0:T(8,128)} custom-call(s32[64]{0:T(128)} %order_ref.1, bf16[128,16384]{1,0:T(8,128)(2,1)} %bitcast.5, bf16[128,1024]{1,0:T(8,128)(2,1)} %bitcast.6, bf16[128,128]{1,0:T(8,128)(2,1)} %bitcast.8, bf16[128,128]{1,0:T(8,128)(2,1)} %bitcast.9, bf16[128,1024]{1,0:T(8,128)(2,1)} %bitcast.7), custom_call_target="tpu_custom_call" | custom-call | tf_op jit(solution)/shard_map/attention_backward_and_weight_gradient/pallas_call | solution.py:601
  191.6 0.0 copy-done.2
  191.6 0.0 copy-done.1
  191.7 0.0 copy-done
  191.7 2.1 %multiply_subtract_fusion = (f32[64,1280]{1,0:T(8,128)}, f32[64,1280]{1,0:T(8,128)}, f32[64,1280]{1,0:T(8,128)}) fusion(f32[64,1280]{1,0:T(8,128)S(1)} %copy-done, f32[64,1280]{1,0:T(8,128)} %attention_backward_and_weight_gradient.1, f32[64,1280]{1,0:T(8,128)S(1)} %copy-done.1, f32[64,1280]{1,0:T(8,128)S(1)} %copy-done.2), kind=kLoop, calls=%fused_computation.2 | loop fusion | flops 1228800 | bytes 2293760 | tf_op jit(solution)/shard_map/sub | solution.py:640
Async XLA Ops:
  0.6 191.0 %copy-start.2 = (f32[64,1280]{1,0:T(8,128)S(1)}, f32[64,1280]{1,0:T(8,128)}, u32[]{:S(2)}) copy-start(f32[64,1280]{1,0:T(8,128)} %param.17) | copy-start | bytes 983044
  0.6 191.0 %copy-start.1 = (f32[64,1280]{1,0:T(8,128)S(1)}, f32[64,1280]{1,0:T(8,128)}, u32[]{:S(2)}) copy-start(f32[64,1280]{1,0:T(8,128)} %param.16) | copy-start | bytes 983044
  0.7 191.0 %copy-start = (f32[64,1280]{1,0:T(8,128)S(1)}, f32[64,1280]{1,0:T(8,128)}, u32[]{:S(2)}) copy-start(f32[64,1280]{1,0:T(8,128)} %param.15) | copy-start | bytes 983044

commit v3 on v2

--- a/solution.py
+++ b/solution.py
@@ -46,6 +46,7 @@
     grad_ref,
     kv_all,
     k_t,
+    x_mid,
     x_recv,
     x_t,
     s_scr,
@@ -69,8 +70,12 @@
     kv1_rs,
     kv2_ss,
     kv2_rs,
-    x_ss,
+    x0_ss,
+    x1_ss,
+    x1_rs,
+    x2_ss,
     x_rs,
+    x_own_sem,
     g1_ss,
     g1_rs,
     g2_ss,
@@ -195,6 +200,63 @@
             piece, piece, kv2_ss.at[z, half, d], kv2_rs.at[z, half, i], line_dev(axis, i)
         )
 
+    def x_columns(half, low, row, col):
+        first = (low * 2 + half) * (NCTX * OWN) + (row * 4 + col) * TOK
+        return x_hbm.at[:, rows(first, TOK)]
+
+    def x_start(half, d):
+        i = line_peer(half, d)
+        for e in range(4):
+            j = lax.rem(place[1 - half] + e, 4)
+            for low in range(4):
+                target = x_recv.at[half, y, x, low] if e == 0 else x_mid.at[half, place[half], j, low]
+                remote(
+                    x_columns(half, low, i, j) if half == 0 else x_columns(half, low, j, i),
+                    target,
+                    x1_ss.at[half, d],
+                    x_rs.at[half, y, x] if e == 0 else x1_rs.at[half, place[half], j],
+                    line_dev(half, i),
+                ).start()
+
+    def x_start_line(half, d):
+        axis = 1 - half
+        i = line_peer(axis, d)
+        for low in range(4):
+            remote(
+                x_columns(half, low, y, i) if half == 0 else x_columns(half, low, i, x),
+                x_recv.at[half, y, x, low],
+                x0_ss.at[half, d],
+                x_rs.at[half, y, x],
+                line_dev(axis, i),
+            ).start()
+
+    def x_own(half, low):
+        return pltpu.make_async_copy(
+            x_columns(half, low, y, x), x_recv.at[half, y, x, low], x_own_sem.at[half, low]
+        )
+
+    def x_two(half, d, e):
+        axis = 1 - half
+        i = line_peer(half, d)
+        j = line_peer(axis, e)
+        where = (i, x) if half == 0 else (y, i)
+        return remote(
+            x_mid.at[half, i, j],
+            x_recv.at[half, where[0], where[1]],
+            x2_ss.at[half, d, e],
+            x_rs.at[half, where[0], where[1]],
+            line_dev(axis, j),
+        )
+
+    def x_forward(half):
+        for d in (1, 3, 2):
+            i = line_peer(half, d)
+            for e in (1, 3, 2):
+                j = line_peer(1 - half, e)
+                piece = x_mid.at[half, i, j]
+                pltpu.make_async_copy(piece, piece, x1_rs.at[half, i, j]).wait()
+                x_two(half, d, e).start()
+
     steps = [(half, d) for d in (1, 3, 2) for half in (0, 1)]
     kvz.start()
     for half, d in steps:
@@ -208,34 +270,24 @@
                 kv_one_arrived(z, half, d).wait_recv()
             for d in (1, 3, 2):
                 kv_two(z, half, d).start()
+    x_start(0, 1)
+    x_start(1, 1)
+    x_start(0, 3)
+    x_start(1, 3)
+    x_start(0, 2)
+    x_start(1, 2)
+    x_start_line(0, 1)
+    x_start_line(1, 1)
+    x_start_line(0, 3)
+    x_start_line(1, 3)
+    x_start_line(0, 2)
+    x_start_line(1, 2)
+    for half in (0, 1):
+        for low in range(4):
+            x_own(half, low).start()
     for z in (z_hi, 1 - z_hi):
         for half, d in steps:
             kv_two_arrived(z, half, d).wait_recv()
-
-    def x_copy(k, j, d):
-        column = ((j % 4) * 2 + j // 4) * (NCTX * OWN) + k * TOK
-        return pltpu.make_async_remote_copy(
-            src_ref=x_hbm.at[:, rows(column, TOK)],
-            dst_ref=x_recv.at[plane, j],
-            send_sem=x_ss.at[d],
-            recv_sem=x_rs.at[plane],
-            device_id=plane_dev(k),
-            device_id_type=MESH,
-        )
-
-    def x_own(j):
-        column = ((j % 4) * 2 + j // 4) * (NCTX * OWN) + plane * TOK
-        return pltpu.make_async_copy(
-            x_hbm.at[:, rows(column, TOK)], x_recv.at[plane, j], x_rs.at[plane]
-        )
-
-    @pl.loop(1, NXY)
-    def _(d):
-        for j in range(8):
-            x_copy(plane_peer(d), j, d).start()
-
-    for j in range(8):
-        x_own(j).start()
 
     lane = lax.broadcasted_iota(jnp.int32, (1, CHUNK), 1)
     token = lax.rem(lane, TOK)
@@ -406,8 +458,13 @@
             for half, d in steps:
                 dkv_first(half, d).start()
         send_chunk(c)
+        if c == 1:
+            x_forward(0)
+            x_forward(1)
         if c > 0:
             forward_chunk(c - 1)
+
+    forward_chunk(3)
 
     for half in (0, 1):
         for d in (1, 3, 2):
@@ -421,8 +478,6 @@
         for d in (1, 3, 2):
             dkv_second(half, d).start()
 
-    forward_chunk(3)
-
     for half in (0, 1):
         axis = 1 - half
         total = dkv_sum[half, place[axis]]
@@ -433,58 +488,57 @@
         zkv_send[1, half] = total[1]
     zkv = remote(zkv_send.at[1 - z_hi], zkv_recv, zkv_ss, zkv_rs, zh_dev)
     zkv.start()
-    zkv.wait_recv()
+
+    def transpose_slot(row, col):
+        for half in (0, 1):
+            for low in range(4):
+                first = (half * 4 + low) * TOK
+                x_t[first : first + TOK, rows((row * 4 + col) * TOK, TOK)] = x_recv[
+                    half, row, col, low
+                ].T
+
     for half in (0, 1):
-        g_all[4, half, y, x] = (zkv_send[z_hi, half] + zkv_recv[half]).astype(BF16)
-    send_chunk(4)
-    forward_chunk(4)
-
-    for j in range(8):
-        x_own(j).wait()
-
-    def transpose_slot(k):
-        for j in range(8):
-            x_t[j * TOK : (j + 1) * TOK, rows(k * TOK, TOK)] = x_recv[k, j].T
-
-    transpose_slot(plane)
+        for low in range(4):
+            x_own(half, low).wait()
+    transpose_slot(y, x)
 
     @pl.loop(1, NXY)
     def _(d):
         k = plane_peer(d)
-        pltpu.make_async_copy(x_recv.at[k], x_recv.at[k], x_rs.at[k]).wait()
-        transpose_slot(k)
+        row, col = k // 4, lax.rem(k, 4)
+        for half in (0, 1):
+            piece = x_recv.at[half, row, col]
+            pltpu.make_async_copy(piece, piece, x_rs.at[half, row, col]).wait()
+        transpose_slot(row, col)
 
     def z_copy(chunk, z, d):
-        return pltpu.make_async_remote_copy(
-            src_ref=z_send.at[chunk, z],
-            dst_ref=z_recv.at[chunk, z_me],
-            send_sem=z_ss.at[chunk, d],
-            recv_sem=z_rs.at[chunk, z_me],
-            device_id=z_dev(z),
-            device_id_type=MESH,
+        return remote(
+            z_send.at[chunk, z],
+            z_recv.at[chunk, z_me],
+            z_ss.at[chunk, d],
+            z_rs.at[chunk, z_me],
+            z_dev(z),
         )
 
     def z_arrived(chunk, z):
-        return pltpu.make_async_remote_copy(
-            src_ref=z_send.at[chunk, z],
-            dst_ref=z_recv.at[chunk, z],
-            send_sem=z_ss.at[chunk, 0],
-            recv_sem=z_rs.at[chunk, z],
-            device_id=z_dev(z),
-            device_id_type=MESH,
+        return remote(
+            z_send.at[chunk, z],
+            z_recv.at[chunk, z],
+            z_ss.at[chunk, 0],
+            z_rs.at[chunk, z],
+            z_dev(z),
         )
 
     def core_copy(chunk):
-        return pltpu.make_async_remote_copy(
-            src_ref=core_send.at[chunk],
-            dst_ref=core_recv.at[chunk],
-            send_sem=core_ss.at[chunk],
-            recv_sem=core_rs.at[chunk],
-            device_id=core_dev,
-            device_id_type=MESH,
-        )
-
-    for c in range(NCHUNK):
+        return remote(
+            core_send.at[chunk],
+            core_recv.at[chunk],
+            core_ss.at[chunk],
+            core_rs.at[chunk],
+            core_dev,
+        )
+
+    def multiply(c):
         for half, d in steps:
             g_two_arrived(c, half, d).wait_recv()
         columns = jnp.concatenate(
@@ -506,6 +560,7 @@
         def _(i):
             half_own[c, rows(i * 256, 256)] = product(core * 512 + i * 256)
 
+    def reduce_cores(c):
         core_copy(c).wait_recv()
         for j in range(NZ):
             z = (j % 2) * 4 + j // 2
@@ -517,6 +572,22 @@
         @pl.loop(1, NZ)
         def _(d):
             z_copy(c, z_peer(d), d).start()
+
+    multiply(0)
+    multiply(1)
+    reduce_cores(0)
+    zkv.wait_recv()
+    for half in (0, 1):
+        g_all[4, half, y, x] = (zkv_send[z_hi, half] + zkv_recv[half]).astype(BF16)
+    send_chunk(4)
+    reduce_cores(1)
+    multiply(2)
+    forward_chunk(4)
+    multiply(3)
+    reduce_cores(2)
+    reduce_cores(3)
+    multiply(4)
+    reduce_cores(4)
 
     for c in range(NCHUNK):
         def add_slot(d, total):
@@ -538,11 +609,10 @@
         for c in range(NCHUNK):
             g_one(c, half, d).wait_send()
             g_two(c, half, d).wait_send()
-
-    @pl.loop(1, NXY)
-    def _(d):
-        k = plane_peer(d)
-        pltpu.make_async_copy(x_recv.at[k], x_recv.at[k], x_ss.at[d]).wait()
+        pltpu.make_async_copy(x_mid.at[0, 0], x_mid.at[0, 0], x1_ss.at[half, d]).wait()
+        pltpu.make_async_copy(x_recv.at[0, 0, 0], x_recv.at[0, 0, 0], x0_ss.at[half, d]).wait()
+        for e in (1, 2, 3):
+            x_two(half, d, e).wait_send()
 
     for c in range(NCHUNK):
         core_copy(c).wait_send()
@@ -558,7 +628,8 @@
     scratch = [
         pltpu.VMEM((2, 4, 4, 2, TOK, HD), BF16),
         pltpu.VMEM((HD, KEYS), BF16),
-        pltpu.VMEM((NXY, 8, TOK, TOK), BF16),
+        pltpu.VMEM((2, 4, 4, 4, TOK, TOK), BF16),
+        pltpu.VMEM((2, 4, 4, 4, TOK, TOK), BF16),
         pltpu.VMEM((ROWS, NXY * TOK), BF16),
         pltpu.VMEM((KEYS, CHUNK), F32),
         pltpu.VMEM((KEYS, CHUNK), F32),
@@ -581,8 +652,12 @@
         dma((2, 2, 4)),
         dma((2, 2, 4)),
         dma((2, 2, 4)),
-        dma((NXY,)),
-        dma((NXY,)),
+        dma((2, 4)),
+        dma((2, 4)),
+        dma((2, 4, 4)),
+        dma((2, 4, 4)),
+        dma((2, 4, 4)),
+        dma((2, 4)),
         dma((NCHUNK, 2, 4)),
         dma((NCHUNK, 2, 4)),
         dma((NCHUNK, 2, 4)),

time: 194 us -> 166 us (0.86)
  Pallas kernels: 191 us -> 162 us
    pallas_call x1, Pallas kernels: 191 us -> 162 us  [fused(): pl.pallas_call(fused_kernel, name='attention_backward_and_weight_gradient...]
where the time goes in v3:
time: 166 us; the launch traced here: 165 us
  Pallas kernels  162 us (98%)
  other arithmetic  2.06 us (1%)
    pallas_call x1, Pallas kernels, fused(): pl.pallas_call(fused_kernel, name='attention_backward_and_weight_gradient...  162 us

profile of v3, /device:TPU:1, one launch (start us, length us, event | category | flops | bytes accessed | tf_op | source)
XLA Modules:
  0.0 164.8 jit_solution(15782672124173975315)
XLA Ops:
  0.6 0.0 copy-start.2
  0.6 0.0 copy-start.1
  0.7 0.0 copy-start
  0.7 162.1 %attention_backward_and_weight_gradient.1 = f32[64,1280]{1,0:T(8,128)} custom-call(s32[64]{0:T(128)} %order_ref.1, bf16[128,16384]{1,0:T(8,128)(2,1)} %bitcast.5, bf16[128,1024]{1,0:T(8,128)(2,1)} %bitcast.6, bf16[128,128]{1,0:T(8,128)(2,1)} %bitcast.8, bf16[128,128]{1,0:T(8,128)(2,1)} %bitcast.9, bf16[128,1024]{1,0:T(8,128)(2,1)} %bitcast.7), custom_call_target="tpu_custom_call" | custom-call | tf_op jit(solution)/shard_map/attention_backward_and_weight_gradient/pallas_call | solution.py:676
  162.7 0.0 copy-done.2
  162.8 0.0 copy-done.1
  162.8 0.0 copy-done
  162.8 2.1 %multiply_subtract_fusion = (f32[64,1280]{1,0:T(8,128)}, f32[64,1280]{1,0:T(8,128)}, f32[64,1280]{1,0:T(8,128)}) fusion(f32[64,1280]{1,0:T(8,128)S(1)} %copy-done, f32[64,1280]{1,0:T(8,128)} %attention_backward_and_weight_gradient.1, f32[64,1280]{1,0:T(8,128)S(1)} %copy-done.1, f32[64,1280]{1,0:T(8,128)S(1)} %copy-done.2), kind=kLoop, calls=%fused_computation.2 | loop fusion | flops 1228800 | bytes 2293760 | tf_op jit(solution)/shard_map/sub | solution.py:715
Async XLA Ops:
  0.6 162.1 %copy-start.2 = (f32[64,1280]{1,0:T(8,128)S(1)}, f32[64,1280]{1,0:T(8,128)}, u32[]{:S(2)}) copy-start(f32[64,1280]{1,0:T(8,128)} %param.17) | copy-start | bytes 983044
  0.6 162.1 %copy-start.1 = (f32[64,1280]{1,0:T(8,128)S(1)}, f32[64,1280]{1,0:T(8,128)}, u32[]{:S(2)}) copy-start(f32[64,1280]{1,0:T(8,128)} %param.16) | copy-start | bytes 983044
  0.7 162.1 %copy-start = (f32[64,1280]{1,0:T(8,128)S(1)}, f32[64,1280]{1,0:T(8,128)}, u32[]{:S(2)}) copy-start(f32[64,1280]{1,0:T(8,128)} %param.15) | copy-start | bytes 983044

commit v4 on v3

--- a/solution.py
+++ b/solution.py
@@ -29,8 +29,10 @@
 NZ = 8
 CHUNK = 256
 NCHUNK = 5
-KEYS = NCTX * TOK
-KT = 512
+KEYS = NXY * TOK
+KT = 256
+SIDE = 256
+LOG2E = math.log2(math.e)
 OWN = 64
 ROWS = 1024
 SCALE = 1.0 / math.sqrt(HD)
@@ -56,16 +58,24 @@
     dkv_one,
     dkv_sum,
     dkv_two,
-    zkv_send,
-    zkv_recv,
+    qo_all,
+    st_send,
+    st_recv,
+    dq_own,
+    dq_send,
+    dq_recv,
     g_all,
     core_send,
     core_recv,
     half_own,
     z_send,
     z_recv,
-    kvz_ss,
-    kvz_rs,
+    qo_ss,
+    qo_rs,
+    st_ss,
+    st_rs,
+    dq_ss,
+    dq_rs,
     kv1_ss,
     kv1_rs,
     kv2_ss,
@@ -84,8 +94,6 @@
     dkv1_rs,
     dkv2_ss,
     dkv2_rs,
-    zkv_ss,
-    zkv_rs,
     core_ss,
     core_rs,
     z_ss,
@@ -152,53 +160,58 @@
     def rows(first, count):
         return pl.ds(pl.multiple_of(first, count), count)
 
-    kv_all[0, y, x, z_hi] = k_ref[...]
-    kv_all[1, y, x, z_hi] = v_ref[...]
+    kv_all[0, y, x] = k_ref[...]
+    kv_all[1, y, x] = v_ref[...]
+    for c in range(4):
+        for i in range(2):
+            head = slice((2 * c + i) * HD, (2 * c + i + 1) * HD)
+            qo_all[c, 0, 0, i * TOK : (i + 1) * TOK] = q_ref[:, head]
+            qo_all[c, 1, 0, i * TOK : (i + 1) * TOK] = o_ref[:, head]
 
     pl.semaphore_wait(barrier, NXY - 1 + NZ - 1 + 1)
 
-    kvz = remote(
-        kv_all.at[:, y, x, z_hi], kv_all.at[:, y, x, z_hi], kvz_ss, kvz_rs, zh_dev
-    )
-
-    def kv_one(z, half, d):
-        piece = kv_all.at[half, y, x, z]
+    def qo_copy(c):
+        return remote(
+            qo_all.at[c, :, 0], qo_all.at[c, :, 1], qo_ss.at[c], qo_rs.at[c], zh_dev
+        )
+
+    def st_copy(c):
+        return remote(st_send.at[c], st_recv.at[c], st_ss.at[c], st_rs.at[c], zh_dev)
+
+    def dq_copy(c):
+        return remote(dq_send.at[c], dq_recv.at[c], dq_ss.at[c], dq_rs.at[c], zh_dev)
+
+    def kv_one(half, d):
+        piece = kv_all.at[half, y, x]
         return remote(
             piece,
             piece,
-            kv1_ss.at[z, half, d],
-            kv1_rs.at[z, half, place[half]],
+            kv1_ss.at[half, d],
+            kv1_rs.at[half, place[half]],
             line_dev(half, line_peer(half, d)),
         )
 
-    def kv_one_arrived(z, half, d):
+    def kv_one_arrived(half, d):
         i = line_peer(half, d)
-        piece = kv_all.at[half, i, x, z] if half == 0 else kv_all.at[half, y, i, z]
-        return remote(
-            piece, piece, kv1_ss.at[z, half, d], kv1_rs.at[z, half, i], line_dev(half, i)
-        )
-
-    def kv_line(z, half, i):
-        return kv_all.at[half, :, i, z] if half == 0 else kv_all.at[half, i, :, z]
-
-    def kv_two(z, half, d):
-        axis = 1 - half
-        piece = kv_line(z, half, place[axis])
+        piece = kv_all.at[half, i, x] if half == 0 else kv_all.at[half, y, i]
+        return remote(piece, piece, kv1_ss.at[half, d], kv1_rs.at[half, i], line_dev(half, i))
+
+    def kv_two(half, d):
+        axis = 1 - half
+        piece = across(kv_all, half, place[axis])
         return remote(
             piece,
             piece,
-            kv2_ss.at[z, half, d],
-            kv2_rs.at[z, half, place[axis]],
+            kv2_ss.at[half, d],
+            kv2_rs.at[half, place[axis]],
             line_dev(axis, line_peer(axis, d)),
         )
 
-    def kv_two_arrived(z, half, d):
+    def kv_two_arrived(half, d):
         axis = 1 - half
         i = line_peer(axis, d)
-        piece = kv_line(z, half, i)
-        return remote(
-            piece, piece, kv2_ss.at[z, half, d], kv2_rs.at[z, half, i], line_dev(axis, i)
-        )
+        piece = across(kv_all, half, i)
+        return remote(piece, piece, kv2_ss.at[half, d], kv2_rs.at[half, i], line_dev(axis, i))
 
     def x_columns(half, low, row, col):
         first = (low * 2 + half) * (NCTX * OWN) + (row * 4 + col) * TOK
@@ -258,18 +271,15 @@
                 x_two(half, d, e).start()
 
     steps = [(half, d) for d in (1, 3, 2) for half in (0, 1)]
-    kvz.start()
     for half, d in steps:
-        kv_one(z_hi, half, d).start()
-    kvz.wait_recv()
-    for half, d in steps:
-        kv_one(1 - z_hi, half, d).start()
-    for z in (z_hi, 1 - z_hi):
-        for half in (0, 1):
-            for d in (1, 3, 2):
-                kv_one_arrived(z, half, d).wait_recv()
-            for d in (1, 3, 2):
-                kv_two(z, half, d).start()
+        kv_one(half, d).start()
+    for c in range(4):
+        qo_copy(c).start()
+    for half in (0, 1):
+        for d in (1, 3, 2):
+            kv_one_arrived(half, d).wait_recv()
+        for d in (1, 3, 2):
+            kv_two(half, d).start()
     x_start(0, 1)
     x_start(1, 1)
     x_start(0, 3)
@@ -285,21 +295,20 @@
     for half in (0, 1):
         for low in range(4):
             x_own(half, low).start()
-    for z in (z_hi, 1 - z_hi):
-        for half, d in steps:
-            kv_two_arrived(z, half, d).wait_recv()
-
-    lane = lax.broadcasted_iota(jnp.int32, (1, CHUNK), 1)
+    for half, d in steps:
+        kv_two_arrived(half, d).wait_recv()
+
+    lane = lax.broadcasted_iota(jnp.int32, (1, 2 * SIDE), 1)
     token = lax.rem(lane, TOK)
-    query_pos = (
-        jnp.where(token < HALF, order_ref[2 * ctx], order_ref[2 * ctx + 1]) * HALF
-        + lax.rem(token, HALF)
-    )
-    sub = lax.broadcasted_iota(jnp.int32, (HALF, CHUNK), 0)
-
-    @pl.loop(0, NCTX)
+    other = plane * 2 + 1 - z_hi
+    first_pos = jnp.where(lane < SIDE, order_ref[2 * ctx], order_ref[2 * other])
+    second_pos = jnp.where(lane < SIDE, order_ref[2 * ctx + 1], order_ref[2 * other + 1])
+    query_pos = jnp.where(token < HALF, first_pos, second_pos) * HALF + lax.rem(token, HALF)
+    sub = lax.broadcasted_iota(jnp.int32, (HALF, 2 * SIDE), 0)
+
+    @pl.loop(0, NXY)
     def _(b):
-        k_t[:, rows(b * TOK, TOK)] = kv_all[0, b // 8, lax.rem(b // 2, 4), lax.rem(b, 2)].T
+        k_t[:, rows(b * TOK, TOK)] = kv_all[0, b // 4, lax.rem(b, 4)].T
 
     def g_one(chunk, half, d):
         piece = g_all.at[chunk, half, y, x]
@@ -396,46 +405,77 @@
     def fold(a, op):
         return op(a.reshape(a.shape[0] // 8, 8, a.shape[1]), axis=0)
 
-    for c in range(4):
-        heads = (2 * c, 2 * c + 1)
-        q_c = jnp.concatenate([q_ref[:, h * HD : (h + 1) * HD] for h in heads], axis=0)
-        o_c = jnp.concatenate([o_ref[:, h * HD : (h + 1) * HD] for h in heads], axis=0)
+    def local_pass(c):
+        slot = c % 2
+        q_c = qo_all[c, 0].reshape(2 * SIDE, HD)
+        o_c = qo_all[c, 1].reshape(2 * SIDE, HD)
 
         def scores_tile(t, top):
             first = pl.multiple_of(t * KT, KT)
             s = lax.dot_general(
-                key_tile(kv_all, 0, t)[...].reshape(KT, HD), q_c, ROW_CONTRACT, preferred_element_type=F32
+                key_tile(kv_all, 0, t)[...].reshape(KT, HD),
+                q_c,
+                ROW_CONTRACT,
+                preferred_element_type=F32,
             )
-            d_scr[pl.ds(first, KT)] = lax.dot_general(
-                key_tile(kv_all, 1, t)[...].reshape(KT, HD), o_c, ROW_CONTRACT, preferred_element_type=F32
+            d_scr[slot, pl.ds(first, KT)] = lax.dot_general(
+                key_tile(kv_all, 1, t)[...].reshape(KT, HD),
+                o_c,
+                ROW_CONTRACT,
+                preferred_element_type=F32,
             )
             for b in range(KT // HALF):
-                limit = query_pos - order_ref[t * (KT // HALF) + b] * HALF
+                owner = (t * 2 + b // 2) * 2 + z_hi
+                limit = query_pos - order_ref[owner * 2 + b % 2] * HALF
                 part = jnp.where(sub <= limit, s[b * HALF : (b + 1) * HALF], NEG_FILL)
-                s_scr[pl.ds(first + b * HALF, HALF)] = part
+                s_scr[slot, pl.ds(first + b * HALF, HALF)] = part
                 top = jnp.maximum(top, fold(part, jnp.max))
             return top
 
-        top = lax.fori_loop(0, KEYS // KT, scores_tile, jnp.full((8, CHUNK), NEG_FILL, F32))
+        top = lax.fori_loop(0, KEYS // KT, scores_tile, jnp.full((8, 2 * SIDE), NEG_FILL, F32))
         top = jnp.max(top, axis=0, keepdims=True)
 
         def weights_tile(t, carried):
             total, inner = carried
             tile = pl.ds(pl.multiple_of(t * KT, KT), KT)
-            e = jnp.exp2((s_scr[tile] - top) * (SCALE * math.log2(math.e)))
-            s_scr[tile] = e
-            return total + fold(e, jnp.sum), inner + fold(e * d_scr[tile], jnp.sum)
-
-        zero = jnp.zeros((8, CHUNK), F32)
+            e = jnp.exp2((s_scr[slot, tile] - top) * (SCALE * LOG2E))
+            s_scr[slot, tile] = e
+            return total + fold(e, jnp.sum), inner + fold(e * d_scr[slot, tile], jnp.sum)
+
+        zero = jnp.zeros((8, 2 * SIDE), F32)
         total, inner = lax.fori_loop(0, KEYS // KT, weights_tile, (zero, zero))
-        inv = 1.0 / jnp.sum(total, axis=0, keepdims=True)
-        delta = jnp.sum(inner, axis=0, keepdims=True) * inv
+        st_send[c, 0:8] = jnp.broadcast_to(top, (8, 2 * SIDE))
+        st_send[c, 8:16] = jnp.broadcast_to(jnp.sum(total, axis=0, keepdims=True), (8, 2 * SIDE))
+        st_send[c, 16:24] = jnp.broadcast_to(jnp.sum(inner, axis=0, keepdims=True), (8, 2 * SIDE))
+        st_copy(c).start()
+
+    def gradient_pass(c):
+        slot = c % 2
+        q_c = qo_all[c, 0].reshape(2 * SIDE, HD)
+        o_c = qo_all[c, 1].reshape(2 * SIDE, HD)
+        st_copy(c).wait_recv()
+
+        def theirs(first):
+            return jnp.concatenate(
+                [
+                    st_recv[c, first : first + 8, SIDE:],
+                    st_recv[c, first : first + 8, :SIDE],
+                ],
+                axis=1,
+            )
+
+        mine_top = st_send[c, 0:8]
+        top = jnp.maximum(mine_top, theirs(0))
+        mine = jnp.exp2((mine_top - top) * (SCALE * LOG2E))
+        other_part = jnp.exp2((theirs(0) - top) * (SCALE * LOG2E))
+        whole = 1.0 / (st_send[c, 8:16] * mine + theirs(8) * other_part)
+        delta = ((st_send[c, 16:24] * mine + theirs(16) * other_part) * whole)[:1]
+        inv = (mine * whole)[:1]
 
         def grads_tile(t, dq):
-            first = pl.multiple_of(t * KT, KT)
-            tile = pl.ds(first, KT)
-            p = s_scr[tile] * inv
-            ds = (p * (d_scr[tile] - delta) * SCALE).astype(BF16)
+            tile = pl.ds(pl.multiple_of(t * KT, KT), KT)
+            p = s_scr[slot, tile] * inv
+            ds = (p * (d_scr[slot, tile] - delta) * SCALE).astype(BF16)
             dk = jnp.dot(ds, q_c, preferred_element_type=F32)
             dv = jnp.dot(p.astype(BF16), o_c, preferred_element_type=F32)
             if c == 0:
@@ -447,24 +487,41 @@
             else:
                 dk = (dkv_acc[tile, :HD] + dk).astype(BF16)
                 dv = (dkv_acc[tile, HD:] + dv).astype(BF16)
-                key_tile(dkv_send, 0, t)[...] = dk.reshape(2, 2, TOK, HD)
-                key_tile(dkv_send, 1, t)[...] = dv.reshape(2, 2, TOK, HD)
+                key_tile(dkv_send, 0, t)[...] = dk.reshape(2, TOK, HD)
+                key_tile(dkv_send, 1, t)[...] = dv.reshape(2, TOK, HD)
             return dq + jnp.dot(k_t[:, tile], ds, preferred_element_type=F32)
 
-        dq = lax.fori_loop(0, KEYS // KT, grads_tile, jnp.zeros((HD, CHUNK), F32))
+        dq = lax.fori_loop(0, KEYS // KT, grads_tile, jnp.zeros((HD, 2 * SIDE), F32))
+        dq_own[c] = dq[:, :SIDE]
+        dq_send[c] = dq[:, SIDE:]
+        dq_copy(c).start()
+
+    def finish_queries(c):
+        dq_copy(c).wait_recv()
         for i in range(2):
-            g_all[c, i, y, x] = dq[:, i * TOK : (i + 1) * TOK].T.astype(BF16)
-        if c == 3:
-            for half, d in steps:
-                dkv_first(half, d).start()
+            part = slice(i * TOK, (i + 1) * TOK)
+            g_all[c, i, y, x] = (dq_own[c, :, part] + dq_recv[c, :, part]).T.astype(BF16)
         send_chunk(c)
-        if c == 1:
+
+    for c in range(4):
+        qo_copy(c).wait_recv()
+        local_pass(c)
+        if c > 0:
+            gradient_pass(c - 1)
+        if c == 2:
             x_forward(0)
             x_forward(1)
-        if c > 0:
-            forward_chunk(c - 1)
-
-    forward_chunk(3)
+        if c > 1:
+            finish_queries(c - 2)
+        if c > 2:
+            forward_chunk(c - 3)
+    gradient_pass(3)
+    for half, d in steps:
+        dkv_first(half, d).start()
+    finish_queries(2)
+    forward_chunk(1)
+    finish_queries(3)
+    forward_chunk(2)
 
     for half in (0, 1):
         for d in (1, 3, 2):
@@ -478,16 +535,16 @@
         for d in (1, 3, 2):
             dkv_second(half, d).start()
 
+    forward_chunk(3)
+
     for half in (0, 1):
         axis = 1 - half
         total = dkv_sum[half, place[axis]]
         for d in (1, 3, 2):
             dkv_second_arrived(half, d).wait_recv()
             total += dkv_two[half, line_peer(axis, d)]
-        zkv_send[0, half] = total[0]
-        zkv_send[1, half] = total[1]
-    zkv = remote(zkv_send.at[1 - z_hi], zkv_recv, zkv_ss, zkv_rs, zh_dev)
-    zkv.start()
+        g_all[4, half, y, x] = total.astype(BF16)
+    send_chunk(4)
 
     def transpose_slot(row, col):
         for half in (0, 1):
@@ -576,10 +633,6 @@
     multiply(0)
     multiply(1)
     reduce_cores(0)
-    zkv.wait_recv()
-    for half in (0, 1):
-        g_all[4, half, y, x] = (zkv_send[z_hi, half] + zkv_recv[half]).astype(BF16)
-    send_chunk(4)
     reduce_cores(1)
     multiply(2)
     forward_chunk(4)
@@ -598,12 +651,13 @@
         own_part = half_own[c, rows((z_lo * 2 + z_hi) * OWN, OWN)]
         grad_ref[:, c * CHUNK : (c + 1) * CHUNK] = lax.fori_loop(1, NZ, add_slot, own_part)
 
-    kvz.wait_send()
-    zkv.wait_send()
+    for c in range(4):
+        qo_copy(c).wait_send()
+        st_copy(c).wait_send()
+        dq_copy(c).wait_send()
     for half, d in steps:
-        for z in (z_hi, 1 - z_hi):
-            kv_one(z, half, d).wait_send()
-            kv_two(z, half, d).wait_send()
+        kv_one(half, d).wait_send()
+        kv_two(half, d).wait_send()
         dkv_first(half, d).wait_send()
         dkv_second(half, d).wait_send()
         for c in range(NCHUNK):
@@ -626,32 +680,40 @@
     vmem = pl.BlockSpec(memory_space=pltpu.VMEM)
     dma = pltpu.SemaphoreType.DMA
     scratch = [
-        pltpu.VMEM((2, 4, 4, 2, TOK, HD), BF16),
+        pltpu.VMEM((2, 4, 4, TOK, HD), BF16),
         pltpu.VMEM((HD, KEYS), BF16),
         pltpu.VMEM((2, 4, 4, 4, TOK, TOK), BF16),
         pltpu.VMEM((2, 4, 4, 4, TOK, TOK), BF16),
         pltpu.VMEM((ROWS, NXY * TOK), BF16),
-        pltpu.VMEM((KEYS, CHUNK), F32),
-        pltpu.VMEM((KEYS, CHUNK), F32),
+        pltpu.VMEM((2, KEYS, 2 * SIDE), F32),
+        pltpu.VMEM((2, KEYS, 2 * SIDE), F32),
         pltpu.VMEM((KEYS, 2 * HD), F32),
-        pltpu.VMEM((2, 4, 4, 2, TOK, HD), BF16),
-        pltpu.VMEM((2, 4, 4, 2, TOK, HD), BF16),
-        pltpu.VMEM((2, 4, 2, TOK, HD), F32),
-        pltpu.VMEM((2, 4, 2, TOK, HD), F32),
-        pltpu.VMEM((2, 2, TOK, HD), F32),
-        pltpu.VMEM((2, TOK, HD), F32),
+        pltpu.VMEM((2, 4, 4, TOK, HD), BF16),
+        pltpu.VMEM((2, 4, 4, TOK, HD), BF16),
+        pltpu.VMEM((2, 4, TOK, HD), F32),
+        pltpu.VMEM((2, 4, TOK, HD), F32),
+        pltpu.VMEM((4, 2, 2, SIDE, HD), BF16),
+        pltpu.VMEM((4, 24, 2 * SIDE), F32),
+        pltpu.VMEM((4, 24, 2 * SIDE), F32),
+        pltpu.VMEM((4, HD, SIDE), F32),
+        pltpu.VMEM((4, HD, SIDE), F32),
+        pltpu.VMEM((4, HD, SIDE), F32),
         pltpu.VMEM((NCHUNK, 2, 4, 4, TOK, HD), BF16),
         pltpu.VMEM((NCHUNK, ROWS // 2, CHUNK), F32),
         pltpu.VMEM((NCHUNK, ROWS // 2, CHUNK), F32),
         pltpu.VMEM((NCHUNK, ROWS // 2, CHUNK), F32),
         pltpu.VMEM((NCHUNK, NZ, OWN, CHUNK), BF16),
         pltpu.VMEM((NCHUNK, NZ, OWN, CHUNK), BF16),
-        dma,
-        dma,
-        dma((2, 2, 4)),
-        dma((2, 2, 4)),
-        dma((2, 2, 4)),
-        dma((2, 2, 4)),
+        dma((4,)),
+        dma((4,)),
+        dma((4,)),
+        dma((4,)),
+        dma((4,)),
+        dma((4,)),
+        dma((2, 4)),
+        dma((2, 4)),
+        dma((2, 4)),
+        dma((2, 4)),
         dma((2, 4)),
         dma((2, 4)),
         dma((2, 4, 4)),
@@ -666,8 +728,6 @@
         dma((2, 4)),
         dma((2, 4)),
         dma((2, 4)),
-        dma,
-        dma,
         dma((NCHUNK,)),
         dma((NCHUNK,)),
         dma((NCHUNK, NZ)),

time: 166 us -> 147 us (0.89)
  Pallas kernels: 162 us -> 144 us
    pallas_call x1, Pallas kernels: 162 us -> 144 us  [fused(): pl.pallas_call(fused_kernel, name='attention_backward_and_weight_gradient...]
where the time goes in v4:
time: 147 us
  Pallas kernels  144 us (98%)
  other arithmetic  2.06 us (1%)
    pallas_call x1, Pallas kernels, fused(): pl.pallas_call(fused_kernel, name='attention_backward_and_weight_gradient...  144 us

profile of v4, /device:TPU:1, one launch (start us, length us, event | category | flops | bytes accessed | tf_op | source)
XLA Modules:
  0.0 146.8 jit_solution(11362170734009305061)
XLA Ops:
  0.6 0.0 copy-start.2
  0.6 0.0 copy-start.1
  0.7 0.0 copy-start
  0.7 144.1 %attention_backward_and_weight_gradient.1 = f32[64,1280]{1,0:T(8,128)} custom-call(s32[64]{0:T(128)} %order_ref.1, bf16[128,16384]{1,0:T(8,128)(2,1)} %bitcast.5, bf16[128,1024]{1,0:T(8,128)(2,1)} %bitcast.6, bf16[128,128]{1,0:T(8,128)(2,1)} %bitcast.8, bf16[128,128]{1,0:T(8,128)(2,1)} %bitcast.9, bf16[128,1024]{1,0:T(8,128)(2,1)} %bitcast.7), custom_call_target="tpu_custom_call" | custom-call | tf_op jit(solution)/shard_map/attention_backward_and_weight_gradient/pallas_call | solution.py:736
  144.8 0.0 copy-done.2
  144.8 0.0 copy-done.1
  144.8 0.0 copy-done
  144.8 2.1 %multiply_subtract_fusion = (f32[64,1280]{1,0:T(8,128)}, f32[64,1280]{1,0:T(8,128)}, f32[64,1280]{1,0:T(8,128)}) fusion(f32[64,1280]{1,0:T(8,128)S(1)} %copy-done, f32[64,1280]{1,0:T(8,128)} %attention_backward_and_weight_gradient.1, f32[64,1280]{1,0:T(8,128)S(1)} %copy-done.1, f32[64,1280]{1,0:T(8,128)S(1)} %copy-done.2), kind=kLoop, calls=%fused_computation.2 | loop fusion | flops 1228800 | bytes 2293760 | tf_op jit(solution)/shard_map/sub | solution.py:775
Async XLA Ops:
  0.6 144.1 %copy-start.2 = (f32[64,1280]{1,0:T(8,128)S(1)}, f32[64,1280]{1,0:T(8,128)}, u32[]{:S(2)}) copy-start(f32[64,1280]{1,0:T(8,128)} %param.17) | copy-start | bytes 983044
  0.6 144.1 %copy-start.1 = (f32[64,1280]{1,0:T(8,128)S(1)}, f32[64,1280]{1,0:T(8,128)}, u32[]{:S(2)}) copy-start(f32[64,1280]{1,0:T(8,128)} %param.16) | copy-start | bytes 983044
  0.7 144.1 %copy-start = (f32[64,1280]{1,0:T(8,128)S(1)}, f32[64,1280]{1,0:T(8,128)}, u32[]{:S(2)}) copy-start(f32[64,1280]{1,0:T(8,128)} %param.15) | copy-start | bytes 983044

commit v5 on v4

--- a/solution.py
+++ b/solution.py
@@ -444,9 +444,10 @@
 
         zero = jnp.zeros((8, 2 * SIDE), F32)
         total, inner = lax.fori_loop(0, KEYS // KT, weights_tile, (zero, zero))
-        st_send[c, 0:8] = jnp.broadcast_to(top, (8, 2 * SIDE))
-        st_send[c, 8:16] = jnp.broadcast_to(jnp.sum(total, axis=0, keepdims=True), (8, 2 * SIDE))
-        st_send[c, 16:24] = jnp.broadcast_to(jnp.sum(inner, axis=0, keepdims=True), (8, 2 * SIDE))
+        row = lax.broadcasted_iota(jnp.int32, (8, 2 * SIDE), 0)
+        total = jnp.sum(total, axis=0, keepdims=True)
+        inner = jnp.sum(inner, axis=0, keepdims=True)
+        st_send[c] = jnp.where(row == 0, top, jnp.where(row == 1, total, inner))
         st_copy(c).start()
 
     def gradient_pass(c):
@@ -455,22 +456,17 @@
         o_c = qo_all[c, 1].reshape(2 * SIDE, HD)
         st_copy(c).wait_recv()
 
-        def theirs(first):
-            return jnp.concatenate(
-                [
-                    st_recv[c, first : first + 8, SIDE:],
-                    st_recv[c, first : first + 8, :SIDE],
-                ],
-                axis=1,
-            )
-
-        mine_top = st_send[c, 0:8]
-        top = jnp.maximum(mine_top, theirs(0))
+        mine_top, mine_total, mine_inner = (st_send[c, r : r + 1] for r in range(3))
+        their_top, their_total, their_inner = (
+            jnp.concatenate([st_recv[c, r : r + 1, SIDE:], st_recv[c, r : r + 1, :SIDE]], axis=1)
+            for r in range(3)
+        )
+        top = jnp.maximum(mine_top, their_top)
         mine = jnp.exp2((mine_top - top) * (SCALE * LOG2E))
-        other_part = jnp.exp2((theirs(0) - top) * (SCALE * LOG2E))
-        whole = 1.0 / (st_send[c, 8:16] * mine + theirs(8) * other_part)
-        delta = ((st_send[c, 16:24] * mine + theirs(16) * other_part) * whole)[:1]
-        inv = (mine * whole)[:1]
+        theirs = jnp.exp2((their_top - top) * (SCALE * LOG2E))
+        whole = 1.0 / (mine_total * mine + their_total * theirs)
+        delta = (mine_inner * mine + their_inner * theirs) * whole
+        inv = mine * whole
 
         def grads_tile(t, dq):
             tile = pl.ds(pl.multiple_of(t * KT, KT), KT)
@@ -508,7 +504,7 @@
         local_pass(c)
         if c > 0:
             gradient_pass(c - 1)
-        if c == 2:
+        if c == 1:
             x_forward(0)
             x_forward(1)
         if c > 1:
@@ -516,35 +512,28 @@
         if c > 2:
             forward_chunk(c - 3)
     gradient_pass(3)
-    for half, d in steps:
-        dkv_first(half, d).start()
-    finish_queries(2)
-    forward_chunk(1)
-    finish_queries(3)
-    forward_chunk(2)
-
-    for half in (0, 1):
-        for d in (1, 3, 2):
-            dkv_first_arrived(half, d).wait_recv()
-        for j in range(4):
-            piece = dkv_send[half, y, j] if half == 0 else dkv_send[half, j, x]
-            total = piece.astype(F32)
+    def sum_first():
+        for half in (0, 1):
             for d in (1, 3, 2):
-                total += dkv_one[half, line_peer(half, d), j].astype(F32)
-            dkv_sum[half, j] = total
-        for d in (1, 3, 2):
-            dkv_second(half, d).start()
-
-    forward_chunk(3)
-
-    for half in (0, 1):
-        axis = 1 - half
-        total = dkv_sum[half, place[axis]]
-        for d in (1, 3, 2):
-            dkv_second_arrived(half, d).wait_recv()
-            total += dkv_two[half, line_peer(axis, d)]
-        g_all[4, half, y, x] = total.astype(BF16)
-    send_chunk(4)
+                dkv_first_arrived(half, d).wait_recv()
+            for j in range(4):
+                piece = dkv_send[half, y, j] if half == 0 else dkv_send[half, j, x]
+                total = piece.astype(F32)
+                for d in (1, 3, 2):
+                    total += dkv_one[half, line_peer(half, d), j].astype(F32)
+                dkv_sum[half, j] = total
+            for d in (1, 3, 2):
+                dkv_second(half, d).start()
+
+    def sum_second():
+        for half in (0, 1):
+            axis = 1 - half
+            total = dkv_sum[half, place[axis]]
+            for d in (1, 3, 2):
+                dkv_second_arrived(half, d).wait_recv()
+                total += dkv_two[half, line_peer(axis, d)]
+            g_all[4, half, y, x] = total.astype(BF16)
+        send_chunk(4)
 
     def transpose_slot(row, col):
         for half in (0, 1):
@@ -554,19 +543,20 @@
                     half, row, col, low
                 ].T
 
-    for half in (0, 1):
-        for low in range(4):
-            x_own(half, low).wait()
-    transpose_slot(y, x)
-
-    @pl.loop(1, NXY)
-    def _(d):
-        k = plane_peer(d)
-        row, col = k // 4, lax.rem(k, 4)
+    def take_input():
         for half in (0, 1):
-            piece = x_recv.at[half, row, col]
-            pltpu.make_async_copy(piece, piece, x_rs.at[half, row, col]).wait()
-        transpose_slot(row, col)
+            for low in range(4):
+                x_own(half, low).wait()
+        transpose_slot(y, x)
+
+        @pl.loop(1, NXY)
+        def _(d):
+            k = plane_peer(d)
+            row, col = k // 4, lax.rem(k, 4)
+            for half in (0, 1):
+                piece = x_recv.at[half, row, col]
+                pltpu.make_async_copy(piece, piece, x_rs.at[half, row, col]).wait()
+            transpose_slot(row, col)
 
     def z_copy(chunk, z, d):
         return remote(
@@ -630,14 +620,24 @@
         def _(d):
             z_copy(c, z_peer(d), d).start()
 
+    for half, d in steps:
+        dkv_first(half, d).start()
+    finish_queries(2)
+    forward_chunk(1)
+    take_input()
     multiply(0)
+    sum_first()
+    reduce_cores(0)
+    finish_queries(3)
+    forward_chunk(2)
     multiply(1)
-    reduce_cores(0)
+    sum_second()
     reduce_cores(1)
+    forward_chunk(3)
     multiply(2)
     forward_chunk(4)
+    reduce_cores(2)
     multiply(3)
-    reduce_cores(2)
     reduce_cores(3)
     multiply(4)
     reduce_cores(4)
@@ -693,8 +693,8 @@
         pltpu.VMEM((2, 4, TOK, HD), F32),
         pltpu.VMEM((2, 4, TOK, HD), F32),
         pltpu.VMEM((4, 2, 2, SIDE, HD), BF16),
-        pltpu.VMEM((4, 24, 2 * SIDE), F32),
-        pltpu.VMEM((4, 24, 2 * SIDE), F32),
+        pltpu.VMEM((4, 8, 2 * SIDE), F32),
+        pltpu.VMEM((4, 8, 2 * SIDE), F32),
         pltpu.VMEM((4, HD, SIDE), F32),
         pltpu.VMEM((4, HD, SIDE), F32),
         pltpu.VMEM((4, HD, SIDE), F32),

time: 147 us -> 134 us (0.912)
  Pallas kernels: 144 us -> 131 us
    pallas_call x1, Pallas kernels: 144 us -> 131 us  [fused(): pl.pallas_call(fused_kernel, name='attention_backward_and_weight_gradient...]
where the time goes in v5:
time: 134 us
  Pallas kernels  131 us (98%)
  other arithmetic  2.06 us (2%)
    pallas_call x1, Pallas kernels, fused(): pl.pallas_call(fused_kernel, name='attention_backward_and_weight_gradient...  131 us

profile of v5, /device:TPU:1, one launch (start us, length us, event | category | flops | bytes accessed | tf_op | source)
XLA Modules:
  0.0 133.7 jit_solution(5440830519105643259)
XLA Ops:
  0.6 0.0 copy-start.2
  0.6 0.0 copy-start.1
  0.7 0.0 copy-start
  0.7 130.9 %attention_backward_and_weight_gradient.1 = f32[64,1280]{1,0:T(8,128)} custom-call(s32[64]{0:T(128)} %order_ref.1, bf16[128,16384]{1,0:T(8,128)(2,1)} %bitcast.5, bf16[128,1024]{1,0:T(8,128)(2,1)} %bitcast.6, bf16[128,128]{1,0:T(8,128)(2,1)} %bitcast.8, bf16[128,128]{1,0:T(8,128)(2,1)} %bitcast.9, bf16[128,1024]{1,0:T(8,128)(2,1)} %bitcast.7), custom_call_target="tpu_custom_call" | custom-call | tf_op jit(solution)/shard_map/attention_backward_and_weight_gradient/pallas_call | solution.py:736
  131.6 0.0 copy-done.2
  131.6 0.0 copy-done.1
  131.6 0.0 copy-done
  131.6 2.1 %multiply_subtract_fusion = (f32[64,1280]{1,0:T(8,128)}, f32[64,1280]{1,0:T(8,128)}, f32[64,1280]{1,0:T(8,128)}) fusion(f32[64,1280]{1,0:T(8,128)S(1)} %copy-done, f32[64,1280]{1,0:T(8,128)} %attention_backward_and_weight_gradient.1, f32[64,1280]{1,0:T(8,128)S(1)} %copy-done.1, f32[64,1280]{1,0:T(8,128)S(1)} %copy-done.2), kind=kLoop, calls=%fused_computation.2 | loop fusion | flops 1228800 | bytes 2293760 | tf_op jit(solution)/shard_map/sub | solution.py:775
Async XLA Ops:
  0.6 130.9 %copy-start.2 = (f32[64,1280]{1,0:T(8,128)S(1)}, f32[64,1280]{1,0:T(8,128)}, u32[]{:S(2)}) copy-start(f32[64,1280]{1,0:T(8,128)} %param.17) | copy-start | bytes 983044
  0.6 130.9 %copy-start.1 = (f32[64,1280]{1,0:T(8,128)S(1)}, f32[64,1280]{1,0:T(8,128)}, u32[]{:S(2)}) copy-start(f32[64,1280]{1,0:T(8,128)} %param.16) | copy-start | bytes 983044
  0.7 130.9 %copy-start = (f32[64,1280]{1,0:T(8,128)S(1)}, f32[64,1280]{1,0:T(8,128)}, u32[]{:S(2)}) copy-start(f32[64,1280]{1,0:T(8,128)} %param.15) | copy-start | bytes 983044

commit v6 on v5

--- a/solution.py
+++ b/solution.py
@@ -624,16 +624,16 @@
         dkv_first(half, d).start()
     finish_queries(2)
     forward_chunk(1)
+    sum_first()
     take_input()
     multiply(0)
-    sum_first()
     reduce_cores(0)
     finish_queries(3)
     forward_chunk(2)
     multiply(1)
     sum_second()
+    forward_chunk(3)
     reduce_cores(1)
-    forward_chunk(3)
     multiply(2)
     forward_chunk(4)
     reduce_cores(2)
@@ -641,15 +641,6 @@
     reduce_cores(3)
     multiply(4)
     reduce_cores(4)
-
-    for c in range(NCHUNK):
-        def add_slot(d, total):
-            z = z_peer(d)
-            z_arrived(c, z).wait_recv()
-            return total + z_recv[c, z].astype(F32)
-
-        own_part = half_own[c, rows((z_lo * 2 + z_hi) * OWN, OWN)]
-        grad_ref[:, c * CHUNK : (c + 1) * CHUNK] = lax.fori_loop(1, NZ, add_slot, own_part)
 
     for c in range(4):
         qo_copy(c).wait_send()
@@ -671,6 +662,16 @@
     for c in range(NCHUNK):
         core_copy(c).wait_send()
 
+    for c in range(NCHUNK):
+        def add_slot(d, total):
+            z = z_peer(d)
+            z_arrived(c, z).wait_recv()
+            return total + z_recv[c, z].astype(F32)
+
+        own_part = half_own[c, rows((z_lo * 2 + z_hi) * OWN, OWN)]
+        grad_ref[:, c * CHUNK : (c + 1) * CHUNK] = lax.fori_loop(1, NZ, add_slot, own_part)
+
+    for c in range(NCHUNK):
         @pl.loop(1, NZ)
         def _(d):
             z_copy(c, z_peer(d), d).wait_send()

time: 134 us -> 132 us (0.985)
    pallas_call x1, Pallas kernels: 131 us -> 130 us  [fused(): pl.pallas_call(fused_kernel, name='attention_backward_and_weight_gradient...]
where the time goes in v6:
time: 132 us
  Pallas kernels  130 us (98%)
  other arithmetic  2.06 us (2%)
    pallas_call x1, Pallas kernels, fused(): pl.pallas_call(fused_kernel, name='attention_backward_and_weight_gradient...  130 us

profile of v6, /device:TPU:1, one launch (start us, length us, event | category | flops | bytes accessed | tf_op | source)
XLA Modules:
  0.0 132.3 jit_solution(17414184023097940527)
XLA Ops:
  0.6 0.0 copy-start.2
  0.6 0.0 copy-start.1
  0.7 0.0 copy-start
  0.7 129.5 %attention_backward_and_weight_gradient.1 = f32[64,1280]{1,0:T(8,128)} custom-call(s32[64]{0:T(128)} %order_ref.1, bf16[128,16384]{1,0:T(8,128)(2,1)} %bitcast.5, bf16[128,1024]{1,0:T(8,128)(2,1)} %bitcast.6, bf16[128,128]{1,0:T(8,128)(2,1)} %bitcast.8, bf16[128,128]{1,0:T(8,128)(2,1)} %bitcast.9, bf16[128,1024]{1,0:T(8,128)(2,1)} %bitcast.7), custom_call_target="tpu_custom_call" | custom-call | tf_op jit(solution)/shard_map/attention_backward_and_weight_gradient/pallas_call | solution.py:737
  130.2 0.0 copy-done.2
  130.2 0.0 copy-done.1
  130.2 0.0 copy-done
  130.2 2.1 %multiply_subtract_fusion = (f32[64,1280]{1,0:T(8,128)}, f32[64,1280]{1,0:T(8,128)}, f32[64,1280]{1,0:T(8,128)}) fusion(f32[64,1280]{1,0:T(8,128)S(1)} %copy-done, f32[64,1280]{1,0:T(8,128)} %attention_backward_and_weight_gradient.1, f32[64,1280]{1,0:T(8,128)S(1)} %copy-done.1, f32[64,1280]{1,0:T(8,128)S(1)} %copy-done.2), kind=kLoop, calls=%fused_computation.2 | loop fusion | flops 1228800 | bytes 2293760 | tf_op jit(solution)/shard_map/sub | solution.py:776
Async XLA Ops:
  0.6 129.6 %copy-start.2 = (f32[64,1280]{1,0:T(8,128)S(1)}, f32[64,1280]{1,0:T(8,128)}, u32[]{:S(2)}) copy-start(f32[64,1280]{1,0:T(8,128)} %param.17) | copy-start | bytes 983044
  0.6 129.6 %copy-start.1 = (f32[64,1280]{1,0:T(8,128)S(1)}, f32[64,1280]{1,0:T(8,128)}, u32[]{:S(2)}) copy-start(f32[64,1280]{1,0:T(8,128)} %param.16) | copy-start | bytes 983044
  0.7 129.6 %copy-start = (f32[64,1280]{1,0:T(8,128)S(1)}, f32[64,1280]{1,0:T(8,128)}, u32[]{:S(2)}) copy-start(f32[64,1280]{1,0:T(8,128)} %param.15) | copy-start | bytes 983044

commit v7 on v6

--- a/solution.py
+++ b/solution.py
@@ -625,10 +625,10 @@
     finish_queries(2)
     forward_chunk(1)
     sum_first()
+    finish_queries(3)
     take_input()
     multiply(0)
     reduce_cores(0)
-    finish_queries(3)
     forward_chunk(2)
     multiply(1)
     sum_second()

time: 132 us -> 133 us (level)
  no operation moved by 1% of the time
where the time goes in v7:
time: 133 us
  Pallas kernels  130 us (98%)
  other arithmetic  2.06 us (2%)
    pallas_call x1, Pallas kernels, fused(): pl.pallas_call(fused_kernel, name='attention_backward_and_weight_gradient...  130 us

profile of v7, /device:TPU:1, one launch (start us, length us, event | category | flops | bytes accessed | tf_op | source)
XLA Modules:
  0.0 132.7 jit_solution(13274240657532456261)
XLA Ops:
  0.6 0.0 copy-start.2
  0.6 0.0 copy-start.1
  0.7 0.0 copy-start
  0.7 129.9 %attention_backward_and_weight_gradient.1 = f32[64,1280]{1,0:T(8,128)} custom-call(s32[64]{0:T(128)} %order_ref.1, bf16[128,16384]{1,0:T(8,128)(2,1)} %bitcast.5, bf16[128,1024]{1,0:T(8,128)(2,1)} %bitcast.6, bf16[128,128]{1,0:T(8,128)(2,1)} %bitcast.8, bf16[128,128]{1,0:T(8,128)(2,1)} %bitcast.9, bf16[128,1024]{1,0:T(8,128)(2,1)} %bitcast.7), custom_call_target="tpu_custom_call" | custom-call | tf_op jit(solution)/shard_map/attention_backward_and_weight_gradient/pallas_call | solution.py:737
  130.6 0.0 copy-done.2
  130.6 0.0 copy-done.1
  130.6 0.0 copy-done
  130.6 2.1 %multiply_subtract_fusion = (f32[64,1280]{1,0:T(8,128)}, f32[64,1280]{1,0:T(8,128)}, f32[64,1280]{1,0:T(8,128)}) fusion(f32[64,1280]{1,0:T(8,128)S(1)} %copy-done, f32[64,1280]{1,0:T(8,128)} %attention_backward_and_weight_gradient.1, f32[64,1280]{1,0:T(8,128)S(1)} %copy-done.1, f32[64,1280]{1,0:T(8,128)S(1)} %copy-done.2), kind=kLoop, calls=%fused_computation.2 | loop fusion | flops 1228800 | bytes 2293760 | tf_op jit(solution)/shard_map/sub | solution.py:776
Async XLA Ops:
  0.6 130.0 %copy-start.2 = (f32[64,1280]{1,0:T(8,128)S(1)}, f32[64,1280]{1,0:T(8,128)}, u32[]{:S(2)}) copy-start(f32[64,1280]{1,0:T(8,128)} %param.17) | copy-start | bytes 983044
  0.6 130.0 %copy-start.1 = (f32[64,1280]{1,0:T(8,128)S(1)}, f32[64,1280]{1,0:T(8,128)}, u32[]{:S(2)}) copy-start(f32[64,1280]{1,0:T(8,128)} %param.16) | copy-start | bytes 983044
  0.7 130.0 %copy-start = (f32[64,1280]{1,0:T(8,128)S(1)}, f32[64,1280]{1,0:T(8,128)}, u32[]{:S(2)}) copy-start(f32[64,1280]{1,0:T(8,128)} %param.15) | copy-start | bytes 983044
